TPU v7x, 128 devices: a whole 4x4x4 slice. The times are simulated.
128 devices in a mesh: row: 4 (over x), pos: 8 (over y_lo, z), batch: 4 (over y_hi, core).
Axes of the slice: x: 4, y: 4 (y_hi: 2, y_lo: 2; y = y_hi * 2 + y_lo), z: 4, core: 2. Of those that a mesh axis runs over, the one named last changes fastest.
Arguments:
- queries: bfloat16 [64, 1024, 768], P(('batch', 'row'), 'pos'), parts along dimension 0, may hold values from -10 to 10
- keys: bfloat16 [64, 1024, 768], P(('batch', 'row'), 'pos'), parts along dimension 0, may hold values from -10 to 10
- values: bfloat16 [64, 1024, 768], P(('batch', 'row'), 'pos'), parts along dimension 0, may hold values from -6 to 6
- out_weight: bfloat16 [768, 768], replicated, may hold values from -0.21875 to 0.21875
- cotangent: bfloat16 [64, 1024, 768], P(('batch', 'row'), 'pos'), parts along dimension 0, may hold values from -6 to 6
- lengths: int32 [64], P(('batch', 'row')), parts along dimension 0, may hold values from 512 to 1024, as said below
Outputs:
- query_grads: bfloat16 [64, 1024, 768], P(('batch', 'row'), 'pos'), parts along dimension 0
- key_grads: bfloat16 [64, 1024, 768], P(('batch', 'row'), 'pos'), parts along dimension 0
- value_grads: bfloat16 [64, 1024, 768], P(('batch', 'row'), 'pos'), parts along dimension 0
- weight_grad: float32 [3072, 768], P('batch'), parts along dimension 0
There are 4 independent parts, one for each index of `batch`. A program takes and returns all parts, laid end to end along the dimension named above; an argument that names none is the same for every part. Nothing has to cross between parts.
Inputs may be any that keep to these rules, and one draw needn't show every extreme that they name: `lengths`: row 0 has length 1024; every row's length is 512 or more.
All inputs are finite; a program needn't handle non-finite values.
Results may differ from a plain program's by a relative error of at most 0.017.
Values may be sent and summed in bfloat16 or wider, within the bound.
A program may use at most 192 MiB of HBM per device.

v0:
```python
import math

import jax
import jax.numpy as jnp
from jax import lax
from jax.sharding import PartitionSpec as P

H = 12
HD = 64


def softmax_back(logit_sum, grad_sum, scale):
    logits = logit_sum * scale
    peak_value = jnp.max(logits, axis=-1, keepdims=True)
    weights = jnp.exp(logits - peak_value)
    probs = weights / jnp.sum(weights, axis=-1, keepdims=True)
    centre = jnp.sum(probs * grad_sum, axis=-1, keepdims=True)
    score_grads = scale * probs * (grad_sum - centre)
    return (probs.astype(jnp.bfloat16), score_grads.astype(jnp.bfloat16))


def per_device(queries, keys, values, out_weight, cotangent, lengths):
    row_count, pos_count, feature_count = queries.shape
    scale = 1.0 / math.sqrt(HD * row_count * lax.axis_size("row"))
    positions = lax.axis_index("pos") * pos_count + jnp.arange(pos_count, dtype=jnp.int32)
    mask = (positions[None, :] < lengths[:, None]).astype(jnp.bfloat16)
    masked = queries * mask[:, :, None]
    flat_cotangent = cotangent.reshape(row_count * pos_count, feature_count)
    d_attended = jnp.einsum(
        "tb,ab->ta", flat_cotangent, out_weight, preferred_element_type=jnp.float32
    )
    d_attended = d_attended.astype(jnp.bfloat16).reshape(row_count, pos_count, H, HD)
    key_all, value_all = (
        lax.all_gather(keys, "pos", axis=1, tiled=True),
        lax.all_gather(values, "pos", axis=1, tiled=True),
    )
    key_count = key_all.shape[1]
    query_four = masked.reshape(row_count, pos_count, H, HD)
    key_four = key_all.reshape(row_count, key_count, H, HD)
    value_four = value_all.reshape(row_count, key_count, H, HD)
    part_logits = jnp.einsum(
        "rihe,rjhe->hij", query_four, key_four, preferred_element_type=jnp.float32
    )
    part_grads = jnp.einsum(
        "rihe,rjhe->hij", d_attended, value_four, preferred_element_type=jnp.float32
    )
    logit_sum, grad_sum = lax.psum((part_logits, part_grads), "row")
    probs, score_grads = softmax_back(logit_sum, grad_sum, scale)
    attended = jnp.einsum("hij,rjhe->rihe", probs, value_four, preferred_element_type=jnp.float32)
    attended = attended.astype(jnp.bfloat16).reshape(row_count * pos_count, feature_count)
    weight_part = jnp.einsum(
        "ta,tb->ab", attended, flat_cotangent, preferred_element_type=jnp.float32
    )
    weight_grad = lax.psum(weight_part, ("row", "pos"))
    mask_float = mask.astype(jnp.float32)
    query_grads = jnp.einsum(
        "hij,rjhe->rihe", score_grads, key_four, preferred_element_type=jnp.float32
    )
    query_grads = (query_grads * mask_float[:, :, None, None]).astype(jnp.bfloat16)
    query_grads = query_grads.reshape(row_count, pos_count, feature_count)
    key_term = jnp.einsum(
        "hij,rihe->rjhe", score_grads, query_four, preferred_element_type=jnp.float32
    )
    value_term = jnp.einsum("hij,rihe->rjhe", probs, d_attended, preferred_element_type=jnp.float32)
    key_term = key_term.reshape(row_count, key_count, feature_count)
    value_term = value_term.reshape(row_count, key_count, feature_count)
    key_sum, value_sum = (
        lax.psum_scatter(
            key_term.astype(jnp.bfloat16), "pos", scatter_dimension=1, tiled=True
        ).astype(jnp.float32),
        lax.psum_scatter(
            value_term.astype(jnp.bfloat16), "pos", scatter_dimension=1, tiled=True
        ).astype(jnp.float32),
    )
    key_grads = key_sum.astype(jnp.bfloat16)
    value_grads = value_sum.astype(jnp.bfloat16)
    return (query_grads, key_grads, value_grads, weight_grad)


def solution(mesh):
    in_specs = (
        P(("batch", "row"), "pos", None),
        P(("batch", "row"), "pos", None),
        P(("batch", "row"), "pos", None),
        P(),
        P(("batch", "row"), "pos", None),
        P(("batch", "row")),
    )
    out_specs = (
        P(("batch", "row"), "pos", None),
        P(("batch", "row"), "pos", None),
        P(("batch", "row"), "pos", None),
        P("batch", None),
    )
    return jax.shard_map(
        per_device, mesh=mesh, in_specs=in_specs, out_specs=out_specs, check_vma=False
    )
```

profile of v0, /device:TPU:16, one launch (start us, length us, event | category | flops | bytes accessed | tf_op | source)
XLA Modules:
  0.0 924.3 jit_solution(15669831018926561427)
XLA Ops:
  7.2 2.4 copy.36
  9.7 0.0 all-gather.3.cloned.1.call-start
  9.7 2.3 copy.34
  12.1 0.0 all-reduce.6.cloned.1.call-start
  12.1 1.5 copy.33
  13.6 0.8 convolution_convert_fusion
  14.5 0.3 copy.35
  14.7 0.2 reshape.100
  15.0 0.1 fusion.17
  15.0 0.1 broadcast_multiply_fusion
  15.1 75.8 %all-gather.5.cloned.1.call-done = bf16[4,1024,768]{1,2,0:T(8,128)(2,1)} async-done(((bf16[4,128,768]{1,2,0:T(8,128)(2,1)}), bf16[4,1024,768]{1,2,0:T(8,128)(2,1)}) %all-gather.5.cloned.1.call-update) | async-done | bytes 6291472 | tf_op jit(solution)/shard_map/all_gather | solution.py:35
  90.9 6.4 convolution_bitcast_fusion
  97.4 75.4 %all-gather.3.cloned.1.call-done = bf16[4,1024,768]{1,2,0:T(8,128)(2,1)} async-done(((bf16[4,128,768]{1,2,0:T(8,128)(2,1)}), bf16[4,1024,768]{1,2,0:T(8,128)(2,1)}) %all-gather.3.cloned.1.call-update) | async-done | bytes 6291472 | tf_op jit(solution)/shard_map/all_gather | solution.py:34
  172.8 6.6 convolution_bitcast_fusion.1
  179.4 229.5 %all-reduce.6.cloned.1.call-done = (f32[12,128,1024]{2,1,0:T(8,128)}, f32[12,128,1024]{2,1,0:T(8,128)}) async-done(((f32[12,128,1024]{2,1,0:T(8,128)}, f32[12,128,1024]{2,1,0:T(8,128)}), (f32[12,128,1024]{2,1,0:T(8,128)}, f32[12,128,1024]{2,1,0:T(8,128)})) %all-reduce.6.cloned.1.call-update) | async-done | bytes 12582928 | tf_op jit(solution)/shard_map/psum | solution.py:47
  408.9 8.9 fusion.27
  417.8 9.6 %convert_bitcast_fusion = bf16[4,1024,12,64]{1,3,0,2:T(8,128)(2,1)} fusion(bf16[4,128,12,64]{1,0,3,2:T(4,128)(2,1)S(1)} %reshape.100, f32[12,128]{1,0:T(8,128)S(1)} %get-tuple-element.16, f32[12,128,1024]{2,1,0:T(8,128)} %get-tuple-element.13), kind=kOutput, calls=%fused_computation.1 | convolution fusion | flops 816318976 | bytes 13375488 | tf_op jit(solution)/shard_map/hij,rihe->rjhe/dot_general | solution.py:64
  427.3 6.6 copy.44
  434.0 10.7 %copy.55 = bf16[4,1024,768]{2,0,1:T(4,128)(2,1)} copy(bf16[4,1024,768]{1,2,0:T(8,128)(2,1)} %bitcast.73) | data formatting | bytes 12582912
  444.7 6.9 copy.60
  451.6 0.2 reduce-scatter.7.cloned.1.call-start
  451.8 5.3 multiply_reduce_fusion
  457.1 1.0 slice-done.1
  458.1 3.8 multiply_convert_fusion
  461.9 1.6 copy-done.2
  463.5 1.8 convert_bitcast_fusion.1
  465.3 3.4 copy.42
  468.7 10.8 %copy.53 = bf16[4,1024,768]{2,0,1:T(4,128)(2,1)} copy(bf16[4,1024,768]{1,2,0:T(8,128)(2,1)} %bitcast.75) | data formatting | bytes 12582912
  479.5 7.0 copy.59
  486.6 6.8 copy.38
  493.4 8.3 fusion.7
  501.7 0.1 convert_bitcast_fusion.2
  501.9 0.6 copy.46
  502.5 2.2 fusion.10
  504.7 3.7 copy.39
  508.5 0.1 copy-done.3
  508.5 1.8 fusion.28
  510.3 0.2 multiply_convert_fusion.1
  510.5 0.1 copy.40
  510.6 1.2 copy.47
  511.8 12.7 %reduce-scatter.9.cloned.1.call-done = bf16[128,3072]{1,0:T(8,128)(2,1)} async-done(((bf16[1024,3072]{1,0:T(8,128)(2,1)}), bf16[128,3072]{1,0:T(8,128)(2,1)}) %reduce-scatter.9.cloned.1.call-update) | async-done | bytes 786448
  524.5 2.0 reshape.115
  526.5 1.0 copy.49
  527.4 71.1 %reduce-scatter.7.cloned.1.call-done = bf16[128,3072]{1,0:T(8,128)(2,1)} async-done(((bf16[1024,3072]{1,0:T(8,128)(2,1)}), bf16[128,3072]{1,0:T(8,128)(2,1)}) %reduce-scatter.7.cloned.1.call-update) | async-done | bytes 786448
  598.5 2.0 reshape.113
  600.5 1.0 copy.48
  601.5 312.8 %all-reduce.4.cloned.1.call-done = f32[768,768]{1,0:T(8,128)} async-done(((f32[768,768]{1,0:T(8,128)}), f32[768,768]{1,0:T(8,128)}) %all-reduce.4.cloned.1.call-update) | async-done | bytes 2359312 | tf_op jit(solution)/shard_map/psum | solution.py:54
  914.3 3.2 copy.77
  (26 shorter events, 0.3 us)
Async XLA Ops:
  7.2 6.5 copy-start
  7.2 6.4 copy-start.4
  7.2 7.7 copy-start.6
  7.2 83.7 %all-gather.5.cloned.1.call-start = ((), (), s32[]{:S(2)}) async-start(), calls=%async_computation.3 | async-start | bytes 7077888 | tf_op jit(solution)/shard_map/all_gather | solution.py:35
  9.7 163.1 %all-gather.3.cloned.1.call-start = ((), (), s32[]{:S(2)}) async-start(), calls=%async_computation.2 | async-start | bytes 7077888 | tf_op jit(solution)/shard_map/all_gather | solution.py:34
  12.1 396.9 %all-reduce.6.cloned.1.call-start = ((), (), s32[]{:S(2)}) async-start(), calls=%async_computation.7 | async-start | bytes 25165824 | tf_op jit(solution)/shard_map/psum | solution.py:47
  179.3 345.1 %reduce-scatter.9.cloned.1.call-start = ((), (), s32[]{:S(2)}) async-start(), calls=%async_computation.6 | async-start | bytes 7077888
  451.5 5.5 slice-start
  451.6 147.0 %reduce-scatter.7.cloned.1.call-start = ((), (), s32[]{:S(2)}) async-start(), calls=%async_computation.5 | async-start | bytes 7077888
  451.8 6.3 slice-start.1
  461.9 1.6 copy-start.2
  486.5 427.8 %all-reduce.4.cloned.1.call-start = ((), (), s32[]{:S(2)}) async-start(), calls=%async_computation.4 | async-start | bytes 4718592 | tf_op jit(solution)/shard_map/psum | solution.py:54
  493.4 9.1 copy-start.5
  504.7 3.8 copy-start.3
  510.6 406.9 %copy-start.1 = (bf16[768,768]{1,0:T(8,128)(2,1)S(1)}, bf16[768,768]{1,0:T(8,128)(2,1)}, u32[]{:S(2)}) copy-start(bf16[768,768]{1,0:T(8,128)(2,1)} %param.9) | copy-start | bytes 3538948
Sparse Core Ops, SparseCore 0:
  10.2 80.6 all-gather.4
  93.1 79.6 all-gather.2
  179.5 229.4 all-reduce.5
  451.7 72.7 reduce-scatter.8
  526.7 71.7 reduce-scatter.6
  601.4 312.7 all-reduce.3
where the time goes:
time: 926 us; the launch traced here: 924 us
  waiting for transfers between devices  777 us (84%)
  local copies, waits for them, and re-layouts  76.3 us (8%)
  matrix products  37.5 us (4%)
  other arithmetic  18.3 us (2%)
  between operations  14.4 us (2%)
    psum x1, waiting for transfers between devices, per_device(): weight_grad = lax.psum(weight_part, ('row', 'pos'))  313 us
    psum x1, waiting for transfers between devices, per_device(): logit_sum, grad_sum = lax.psum((part_logits, part_grads), 'row')  230 us
    unnamed x8, waiting for transfers between devices  83.9 us
    all_gather x1, waiting for transfers between devices, per_device(): lax.all_gather(values, 'pos', axis=1, tiled=True)  75.8 us
    all_gather x1, waiting for transfers between devices, per_device(): lax.all_gather(keys, 'pos', axis=1, tiled=True)  75.4 us
    unnamed x31, local copies, waits for them, and re-layouts  54.6 us
  transfers between devices with their start and end apart: 6, of which 6 were waited for; matrix products, arithmetic and copies ran while one was open for 8% of the time, Pallas kernels for 0%

commit v1 on v0

v1 whole, which is shorter than its diff:
```python
import math

import jax
import jax.numpy as jnp
from jax import lax
from jax.experimental import pallas as pl
from jax.experimental.pallas import tpu as pltpu
from jax.sharding import PartitionSpec as P

H = 12
HD = 64
D = 768
ROWS = 4
POS = 128
NX = 4
NP = 8
ND = NX * NP
L = POS * NP
TILE = ROWS * HD
WIDE = TILE * NX
SLICE = D * D // 128 // ND
HEADS_X = H // NX
MESH = pl.DeviceIdType.MESH
F32 = jnp.float32
BF16 = jnp.bfloat16

K_, Q_, V_, A_ = range(4)
AT_, VG_, QG_, KG_ = range(4)


def swap_pair(first, second, low):
    first_r = jnp.concatenate([first[:, HD:], first[:, :HD]], axis=1)
    second_r = jnp.concatenate([second[:, HD:], second[:, :HD]], axis=1)
    return jnp.where(low, first, second_r), jnp.where(low, first_r, second)


def kernel(
    lengths, q_hbm, k_hbm, v_hbm, c_hbm, w_hbm,
    qg_hbm, kg_hbm, vg_hbm, wg_hbm,
    q_in, k_in, v_in, c_in, w_in, stage, full, probs, probs_b, scores, outs, back,
    att, w_send, w_recv, w_mine, w_all, w_out,
    load_sem, in_send, in_recv, out_send, out_recv, w_send_sem, w_recv_sem, store_sem,
):
    x = lax.axis_index("row")
    p = lax.axis_index("pos")
    core = lax.rem(lax.axis_index("batch"), 2)
    me = x * NP + p
    turn = lax.rem(lax.rem(p, 4) + 4 - x, 4)
    own_k = lax.rem(turn * 2, 3)
    owner = jnp.logical_and(turn < 3, p // 4 == lax.rem(own_k // 2 + core, 2))
    head = HEADS_X * x + own_k

    def owner_of(h):
        hx, hk = h // HEADS_X, lax.rem(h, HEADS_X)
        return hx, lax.rem(hk // 2 + core, 2) * 4 + lax.rem(lax.rem(2 * hk, 3) + hx, 4)

    def device(dx, dp):
        return {"row": dx, "pos": dp}

    loads = [
        pltpu.make_async_copy(src, dst, load_sem.at[i])
        for i, (src, dst) in enumerate(
            ((k_hbm, k_in), (q_hbm, q_in), (v_hbm, v_in), (c_hbm, c_in), (w_hbm, w_in))
        )
    ]
    for load in loads:
        load.start()

    barrier = pltpu.get_barrier_semaphore()

    def greet(i, carry):
        other = lax.rem(me + i, ND)
        pl.semaphore_signal(
            barrier, inc=1, device_id=device(other // NP, lax.rem(other, NP)), device_id_type=MESH
        )
        return carry

    lax.fori_loop(1, ND, greet, 0)

    low = lax.broadcasted_iota(jnp.int32, (POS, 2 * HD), 1) < HD
    spots = p * POS + lax.broadcasted_iota(jnp.int32, (POS, 2 * HD), 0)

    def to_heads(t, rows_of, tiles):
        for c in tiles:
            for half in range(2):
                even, odd = swap_pair(rows_of(2 * half, c), rows_of(2 * half + 1, c), low)
                lanes = slice(half * 128, half * 128 + 128)
                stage[t, 2 * c, :, lanes] = even
                stage[t, 2 * c + 1, :, lanes] = odd

    def send_heads(t):
        def body(i, carry):
            h = lax.rem(i + HEADS_X * x, H)
            hx, hp = owner_of(h)
            place = full.at[
                t, pl.ds(pl.multiple_of(p * POS, POS), POS), pl.ds(pl.multiple_of(x * TILE, TILE), TILE)
            ]
            mine = jnp.logical_and(hx == x, hp == p)

            @pl.when(mine)
            def _():
                pltpu.make_async_copy(stage.at[t, h], place, in_recv.at[t]).start()

            @pl.when(jnp.logical_not(mine))
            def _():
                pltpu.make_async_remote_copy(
                    stage.at[t, h], place, in_send.at[t], in_recv.at[t],
                    device_id=device(hx, hp), device_id_type=MESH,
                ).start()

            return carry

        lax.fori_loop(0, H, body, 0)

    tiles = range(H // 2)
    loads[0].wait()
    to_heads(K_, lambda r, c: k_in[r, :, c * 128 : c * 128 + 128], tiles)
    pl.semaphore_wait(barrier, ND - 1)
    send_heads(K_)
    loads[1].wait()
    to_heads(
        Q_,
        lambda r, c: jnp.where(
            spots < lengths[r], q_in[r, :, c * 128 : c * 128 + 128], jnp.zeros((), BF16)
        ),
        tiles,
    )
    send_heads(Q_)
    loads[2].wait()
    to_heads(V_, lambda r, c: v_in[r, :, c * 128 : c * 128 + 128], tiles)
    send_heads(V_)
    loads[3].wait()
    loads[4].wait()
    for block in range(3):
        part = lax.dot_general(
            c_in[...].reshape(ROWS * POS, D), w_in[block * 256 : block * 256 + 256, :],
            (((1,), (1,)), ((), ())), preferred_element_type=F32,
        ).astype(BF16)
        to_heads(
            A_,
            lambda r, c: part[r * POS : r * POS + POS, (c - 2 * block) * 128 : (c - 2 * block) * 128 + 128],
            (2 * block, 2 * block + 1),
        )
    send_heads(A_)

    scale = 1.0 / math.sqrt(HD * ROWS * NX)
    step = 256

    def arrived(t):
        pltpu.make_async_copy(full.at[t], full.at[t], in_recv.at[t]).wait()

    def send_back(t, block):
        def body(i, carry):
            dx = lax.rem(x + lax.rem(i, NX), NX)
            dp = block * 2 + i // NX
            src = outs.at[
                t, pl.ds(pl.multiple_of(dp * POS, POS), POS), pl.ds(pl.multiple_of(dx * TILE, TILE), TILE)
            ]
            mine = jnp.logical_and(dx == x, dp == p)

            @pl.when(mine)
            def _():
                pltpu.make_async_copy(src, back.at[t, head], out_recv.at[t]).start()

            @pl.when(jnp.logical_not(mine))
            def _():
                pltpu.make_async_remote_copy(
                    src, back.at[t, head], out_send.at[t], out_recv.at[t],
                    device_id=device(dx, dp), device_id_type=MESH,
                ).start()

            return carry

        lax.fori_loop(0, 2 * NX, body, 0)

    def rows_at(i, size=step):
        return pl.ds(pl.multiple_of(i * size, size), size)

    def back_here(t):
        pltpu.make_async_copy(back.at[t], back.at[t], out_recv.at[t]).wait()

    def from_heads(t, store):
        for c in tiles:
            for half in range(2):
                lanes = slice(half * 128, half * 128 + 128)
                one, two = swap_pair(back[t, 2 * c, :, lanes], back[t, 2 * c + 1, :, lanes], low)
                store(2 * half, c, one)
                store(2 * half + 1, c, two)

    @pl.when(owner)
    def _():
        arrived(K_)
        arrived(Q_)

        def softmax(i, carry):
            rows = rows_at(i, POS)
            logits = lax.dot_general(
                full[Q_, rows, :], full[K_], (((1,), (1,)), ((), ())), preferred_element_type=F32
            ) * scale
            weights = jnp.exp(logits - jnp.max(logits, axis=-1, keepdims=True))
            result = weights / jnp.sum(weights, axis=-1, keepdims=True)
            probs[rows, :] = result
            probs_b[rows, :] = result.astype(BF16)
            return carry

        lax.fori_loop(0, L // POS, softmax, 0)
        arrived(V_)

        def attend(i, carry):
            rows = rows_at(i)
            outs[AT_, rows, :] = jnp.dot(
                probs_b[rows, :], full[V_], preferred_element_type=F32
            ).astype(BF16)
            send_back(AT_, i)
            return carry

        lax.fori_loop(0, L // step, attend, 0)
        arrived(A_)

        def value_grad(i, carry):
            rows = rows_at(i)
            outs[VG_, rows, :] = lax.dot_general(
                probs_b[:, rows], full[A_], (((0,), (0,)), ((), ())), preferred_element_type=F32
            ).astype(BF16)
            send_back(VG_, i)
            return carry

        lax.fori_loop(0, L // step, value_grad, 0)

        def score_grad(i, carry):
            rows = rows_at(i, POS)
            grads = lax.dot_general(
                full[A_, rows, :], full[V_], (((1,), (1,)), ((), ())), preferred_element_type=F32
            )
            prob = probs[rows, :]
            centre = jnp.sum(prob * grads, axis=-1, keepdims=True)
            scores[rows, :] = (scale * prob * (grads - centre)).astype(BF16)
            return carry

        lax.fori_loop(0, L // POS, score_grad, 0)

        def query_grad(i, carry):
            rows = rows_at(i)
            outs[QG_, rows, :] = jnp.dot(
                scores[rows, :], full[K_], preferred_element_type=F32
            ).astype(BF16)
            send_back(QG_, i)
            return carry

        lax.fori_loop(0, L // step, query_grad, 0)

    back_here(AT_)

    def store_att(r, c, tile):
        att[r, :, c * 128 : c * 128 + 128] = tile

    from_heads(AT_, store_att)
    for block in range(3):
        part = lax.dot_general(
            att[...].reshape(ROWS * POS, D),
            c_in[:, :, block * 256 : block * 256 + 256].reshape(ROWS * POS, 256),
            (((0,), (0,)), ((), ())), preferred_element_type=F32,
        ).astype(BF16)
        w_send[2 * block * D : 2 * block * D + D, :] = part[:, :128]
        w_send[2 * block * D + D : 2 * block * D + 2 * D, :] = part[:, 128:]

    def scatter(i, carry):
        other = lax.rem(me + i, ND)
        pltpu.make_async_remote_copy(
            w_send.at[pl.ds(pl.multiple_of(other * SLICE, 16), SLICE)], w_recv.at[me],
            w_send_sem.at[0], w_recv_sem.at[0],
            device_id=device(other // NP, lax.rem(other, NP)), device_id_type=MESH,
        ).start()
        return carry

    lax.fori_loop(1, ND, scatter, 0)
    pltpu.make_async_copy(
        w_send.at[pl.ds(pl.multiple_of(me * SLICE, 16), SLICE)], w_recv.at[me], w_recv_sem.at[0]
    ).start()

    @pl.when(owner)
    def _():
        def key_grad(i, carry):
            rows = rows_at(i)
            outs[KG_, rows, :] = lax.dot_general(
                scores[:, rows], full[Q_], (((0,), (0,)), ((), ())), preferred_element_type=F32
            ).astype(BF16)
            send_back(KG_, i)
            return carry

        lax.fori_loop(0, L // step, key_grad, 0)

    pltpu.make_async_copy(w_recv, w_recv, w_recv_sem.at[0]).wait()
    total = w_recv[0].astype(F32)
    for i in range(1, ND):
        total = total + w_recv[i].astype(F32)
    w_mine[...] = total.astype(BF16)

    def spread(i, carry):
        other = lax.rem(me + i, ND)
        pltpu.make_async_remote_copy(
            w_mine, w_all.at[pl.ds(pl.multiple_of(me * SLICE, 16), SLICE)],
            w_send_sem.at[1], w_recv_sem.at[1],
            device_id=device(other // NP, lax.rem(other, NP)), device_id_type=MESH,
        ).start()
        return carry

    lax.fori_loop(1, ND, spread, 0)
    pltpu.make_async_copy(
        w_mine, w_all.at[pl.ds(pl.multiple_of(me * SLICE, 16), SLICE)], w_recv_sem.at[1]
    ).start()

    def finish(t, result, hbm, sem, masked=False):
        back_here(t)

        def store(r, c, tile):
            if masked:
                tile = jnp.where(spots < lengths[r], tile, jnp.zeros((), BF16))
            result[r, :, c * 128 : c * 128 + 128] = tile

        from_heads(t, store)
        copy = pltpu.make_async_copy(result, hbm, store_sem.at[sem])
        copy.start()
        return copy

    stores = [
        finish(VG_, v_in, vg_hbm, 0),
        finish(QG_, q_in, qg_hbm, 1, masked=True),
        finish(KG_, k_in, kg_hbm, 2),
    ]
    pltpu.make_async_copy(w_all, w_all, w_recv_sem.at[1]).wait()
    for c in range(D // 128):
        w_out[:, c * 128 : c * 128 + 128] = w_all[c * D : c * D + D, :].astype(F32)
    stores.append(pltpu.make_async_copy(w_out, wg_hbm, store_sem.at[3]))
    stores[-1].start()
    for store in stores:
        store.wait()

    for t in range(4):
        @pl.when(owner)
        def _():
            sent = stage.at[t, pl.ds(0, H - 1)]
            pltpu.make_async_copy(sent, sent, in_send.at[t]).wait()
            given = outs.at[t, pl.ds(0, L - L // ND)]
            pltpu.make_async_copy(given, given, out_send.at[t]).wait()

        @pl.when(jnp.logical_not(owner))
        def _():
            pltpu.make_async_copy(stage.at[t], stage.at[t], in_send.at[t]).wait()

    for i in range(2):
        sent = w_send.at[pl.ds(0, (ND - 1) * SLICE)]
        pltpu.make_async_copy(sent, sent, w_send_sem.at[i]).wait()


def per_device(queries, keys, values, out_weight, cotangent, lengths):
    any_space = pl.BlockSpec(memory_space=pl.ANY)
    local = jax.ShapeDtypeStruct((ROWS, POS, D), BF16)
    vmem = pltpu.VMEM
    dma = pltpu.SemaphoreType.DMA
    return pl.pallas_call(
        kernel,
        out_shape=(local, local, local, jax.ShapeDtypeStruct((D, D), F32)),
        in_specs=[pl.BlockSpec(memory_space=pltpu.SMEM)] + [any_space] * 5,
        out_specs=(any_space,) * 4,
        scratch_shapes=[
            vmem((ROWS, POS, D), BF16),
            vmem((ROWS, POS, D), BF16),
            vmem((ROWS, POS, D), BF16),
            vmem((ROWS, POS, D), BF16),
            vmem((D, D), BF16),
            vmem((4, H, POS, TILE), BF16),
            vmem((4, L, WIDE), BF16),
            vmem((L, L), F32),
            vmem((L, L), BF16),
            vmem((L, L), BF16),
            vmem((4, L, WIDE), BF16),
            vmem((4, H, POS, TILE), BF16),
            vmem((ROWS, POS, D), BF16),
            vmem((ND * SLICE, 128), BF16),
            vmem((ND, SLICE, 128), BF16),
            vmem((SLICE, 128), BF16),
            vmem((ND * SLICE, 128), BF16),
            vmem((D, D), F32),
            dma((5,)), dma((4,)), dma((4,)), dma((4,)), dma((4,)), dma((2,)), dma((2,)), dma((4,)),
        ],
        compiler_params=pltpu.CompilerParams(
            collective_id=0, has_side_effects=True, vmem_limit_bytes=58 * 2**20
        ),
        cost_estimate=pl.CostEstimate(
            flops=14 * L**3, bytes_accessed=12 * 2**20, transcendentals=L * L
        ),
    )(lengths, queries, keys, values, cotangent, out_weight)


def solution(mesh):
    tokens = P(("batch", "row"), "pos", None)
    return jax.shard_map(
        per_device,
        mesh=mesh,
        in_specs=(tokens, tokens, tokens, P(), tokens, P(("batch", "row"))),
        out_specs=(tokens, tokens, tokens, P("batch", None)),
        check_vma=False,
    )
```

time: 926 us -> 154 us (0.17)
  waiting for transfers between devices: 777 us -> 0 us
  Pallas kernels: 0 us -> 145 us
  local copies, waits for them, and re-layouts: 76.3 us -> 6.57 us
  matrix products: 37.5 us -> 0 us
  other arithmetic: 18.3 us -> 0 us
  between operations: 14.4 us -> 0.66 us
    psum x2 -> x0, waiting for transfers between devices: 542 us -> none  [the longest x1 313 us: per_device(): weight_grad = lax.psum(weight_part, ('row', 'pos'))]
    all_gather x2 -> x0, waiting for transfers between devices: 151 us -> none  [the longest x1 75.8 us: per_device(): lax.all_gather(values, 'pos', axis=1, tiled=True)]
    pallas_call x0 -> x1, Pallas kernels: none -> 145 us  [per_device(): pl.pallas_call(kernel, out_shape=(local, local, local, jax.ShapeDtypeStru...]
    unnamed x8 -> x0, waiting for transfers between devices: 83.9 us -> none
    unnamed x31 -> x8, local copies, waits for them, and re-layouts: 54.6 us -> 6.57 us
    dot_general x6 -> x0, matrix products: 27.3 us -> none  [the longest x1 9.56 us: per_device(): jnp.einsum('hij,rihe->rjhe', probs, d_attended, preferred_element_type=jn...]
    convert_element_type x5 -> x0, local copies, waits for them, and re-layouts: 11 us -> none  [the longest x1 6.63 us: per_device(): value_term.astype(jnp.bfloat16)]
    reshape x3 -> x0, local copies, waits for them, and re-layouts: 10.7 us -> none  [the longest x1 6.8 us: per_device(): value_four = value_all.reshape(row_count, key_count, H, HD)]
  transfers between devices with their start and end apart: 6 -> 0, of which waited for: 6 -> 0; matrix products, arithmetic and copies ran while one was open for 8% -> 0% of each run, Pallas kernels for 0% -> 0%
where the time goes in v1:
time: 154 us; the launch traced here: 152 us
  Pallas kernels  145 us (94%)
  local copies, waits for them, and re-layouts  6.57 us (4%)
    pallas_call x1, Pallas kernels, per_device(): pl.pallas_call(kernel, out_shape=(local, local, local, jax.ShapeDtypeStru...  145 us
    unnamed x8, local copies, waits for them, and re-layouts  6.57 us

profile of v1, /device:TPU:16, one launch (start us, length us, event | category | flops | bytes accessed | tf_op | source)
XLA Modules:
  0.0 152.4 jit_solution(3689794035355852101)
XLA Ops:
  0.6 145.1 %shard_map.93 = (bf16[4,128,768]{2,1,0:T(8,128)(2,1)}, bf16[4,128,768]{2,1,0:T(8,128)(2,1)}, bf16[4,128,768]{2,1,0:T(8,128)(2,1)}, f32[768,768]{1,0:T(8,128)}) custom-call(s32[4]{0:T(128)} %lengths.1, bf16[4,128,768]{2,1,0:T(8,128)(2,1)} %q_hbm.1, bf16[4,128,768]{2,1,0:T(8,128)(2,1)} %k_hbm.1, bf16[4,128,768]{2,1,0:T(8,128)(2,1)} %v_hbm.1, ...), custom_call_target="tpu_custom_call" | custom-call | flops 15032385536 | bytes 12582912 | tf_op jit(solution)/shard_map/pallas_call | solution.py:361
  145.8 0.0 copy-start.1
  145.8 0.0 copy-start
  145.8 2.2 %copy.14 = bf16[4,128,768]{2,1,0:T(8,128)(2,1)} copy(bf16[4,128,768]{2,1,0:T(8,128)(2,1)} %get-tuple-element.8) | data formatting | bytes 1572864
  148.0 2.1 %copy.15 = bf16[4,128,768]{2,1,0:T(8,128)(2,1)} copy(bf16[4,128,768]{2,1,0:T(8,128)(2,1)} %get-tuple-element.9) | data formatting | bytes 1572864
  150.1 0.0 copy-done.1
  150.1 0.9 copy.16
  150.9 0.0 copy-done
  150.9 1.4 copy.17
Async XLA Ops:
  145.8 4.3 %copy-start.1 = (bf16[4,128,768]{2,1,0:T(8,128)(2,1)S(1)}, bf16[4,128,768]{2,1,0:T(8,128)(2,1)}, u32[]{:S(2)}) copy-start(bf16[4,128,768]{2,1,0:T(8,128)(2,1)} %get-tuple-element.10) | copy-start | bytes 2359300
  145.8 5.2 %copy-start = (f32[768,768]{1,0:T(8,128)S(1)}, f32[768,768]{1,0:T(8,128)}, u32[]{:S(2)}) copy-start(f32[768,768]{1,0:T(8,128)} %get-tuple-element.11) | copy-start | bytes 7077892

commit v2 on v1

--- a/solution.py
+++ b/solution.py
@@ -36,10 +36,11 @@
 
 def kernel(
     lengths, q_hbm, k_hbm, v_hbm, c_hbm, w_hbm,
-    qg_hbm, kg_hbm, vg_hbm, wg_hbm,
-    q_in, k_in, v_in, c_in, w_in, stage, full, probs, probs_b, scores, outs, back,
-    att, w_send, w_recv, w_mine, w_all, w_out,
-    load_sem, in_send, in_recv, out_send, out_recv, w_send_sem, w_recv_sem, store_sem,
+    back, w_all,
+    q_in, k_in, v_in, c_in, w_in, stage, full, probs, probs_b, scores, outs, back_att,
+    att, w_send, w_recv, w_mine, relay_in, relay_out,
+    load_sem, in_send, in_recv, out_send, out_recv, w_send_sem, w_recv_sem,
+    relay_send, relay_recv, relay_out_send, relay_out_recv,
 ):
     x = lax.axis_index("row")
     p = lax.axis_index("pos")
@@ -57,6 +58,26 @@
     def device(dx, dp):
         return {"row": dx, "pos": dp}
 
+    y, z = p // 4, lax.rem(p, 4)
+
+    def helper_y(dz):
+        return lax.rem(1 - core + (lax.rem(dz + 4 - x, 4) == 1).astype(jnp.int32), 2)
+
+    helped_in = y == helper_y(3 - z)
+    helper_in = y == helper_y(z)
+
+    def slot_owner(oz, slot):
+        hx = lax.rem(oz + 4 - slot, 4)
+        h = HEADS_X * hx + lax.rem(2 * slot, 3)
+        return h, hx, owner_of(h)[1]
+
+    giver_x = lax.rem(x + 2 * lax.rem(x, 2) + 3, 4)
+    giver_turn = lax.rem(z + 4 - giver_x, 4)
+    giver_k = lax.rem(giver_turn * 2, 3)
+    helper_out = jnp.logical_and(
+        giver_turn < 3, y == lax.rem(giver_k // 2 + core, 2)
+    )
+
     loads = [
         pltpu.make_async_copy(src, dst, load_sem.at[i])
         for i, (src, dst) in enumerate(
@@ -89,9 +110,24 @@
                 stage[t, 2 * c + 1, :, lanes] = odd
 
     def send_heads(t):
+        @pl.when(helped_in)
+        def _():
+            def hand(slot, carry):
+                h, _, _ = slot_owner(lax.rem(z + 2, 4), slot)
+                pltpu.make_async_remote_copy(
+                    stage.at[t, h], relay_in.at[t, slot], in_send.at[t], relay_recv.at[t],
+                    device_id=device(x, y * 4 + 3 - z), device_id_type=MESH,
+                ).start()
+                return carry
+
+            lax.fori_loop(0, 3, hand, 0)
+
         def body(i, carry):
             h = lax.rem(i + HEADS_X * x, H)
             hx, hp = owner_of(h)
+            direct = jnp.logical_not(
+                jnp.logical_and(helped_in, lax.rem(hp, 4) == lax.rem(z + 2, 4))
+            )
             place = full.at[
                 t, pl.ds(pl.multiple_of(p * POS, POS), POS), pl.ds(pl.multiple_of(x * TILE, TILE), TILE)
             ]
@@ -101,7 +137,7 @@
             def _():
                 pltpu.make_async_copy(stage.at[t, h], place, in_recv.at[t]).start()
 
-            @pl.when(jnp.logical_not(mine))
+            @pl.when(jnp.logical_and(direct, jnp.logical_not(mine)))
             def _():
                 pltpu.make_async_remote_copy(
                     stage.at[t, h], place, in_send.at[t], in_recv.at[t],
@@ -111,6 +147,25 @@
             return carry
 
         lax.fori_loop(0, H, body, 0)
+
+    def hand_on_in(t):
+        @pl.when(helper_in)
+        def _():
+            pltpu.make_async_copy(relay_in.at[t], relay_in.at[t], relay_recv.at[t]).wait()
+
+            def hand(slot, carry):
+                _, hx, hp = slot_owner(z + 1 - 2 * lax.rem(z, 2), slot)
+                place = full.at[
+                    t, pl.ds(pl.multiple_of((y * 4 + 3 - z) * POS, POS), POS),
+                    pl.ds(pl.multiple_of(x * TILE, TILE), TILE),
+                ]
+                pltpu.make_async_remote_copy(
+                    relay_in.at[t, slot], place, relay_send.at[t], in_recv.at[t],
+                    device_id=device(hx, hp), device_id_type=MESH,
+                ).start()
+                return carry
+
+            lax.fori_loop(0, 3, hand, 0)
 
     tiles = range(H // 2)
     loads[0].wait()
@@ -126,9 +181,11 @@
         tiles,
     )
     send_heads(Q_)
+    hand_on_in(K_)
     loads[2].wait()
     to_heads(V_, lambda r, c: v_in[r, :, c * 128 : c * 128 + 128], tiles)
     send_heads(V_)
+    hand_on_in(Q_)
     loads[3].wait()
     loads[4].wait()
     for block in range(3):
@@ -142,12 +199,31 @@
             (2 * block, 2 * block + 1),
         )
     send_heads(A_)
+    hand_on_in(V_)
+    hand_on_in(A_)
 
     scale = 1.0 / math.sqrt(HD * ROWS * NX)
     step = 256
 
     def arrived(t):
         pltpu.make_async_copy(full.at[t], full.at[t], in_recv.at[t]).wait()
+
+    def place_of(t, h):
+        return back_att.at[h] if t == AT_ else back.at[t - 1, h]
+
+    def hand_on_out(t):
+        @pl.when(helper_out)
+        def _():
+            def hand(block, carry):
+                tile = relay_out.at[t, block]
+                pltpu.make_async_copy(tile, tile, relay_out_recv.at[t, block]).wait()
+                pltpu.make_async_remote_copy(
+                    tile, place_of(t, HEADS_X * giver_x + giver_k), relay_out_send.at[t], out_recv.at[t],
+                    device_id=device(lax.rem(giver_x + 2, 4), 2 * block + 1), device_id_type=MESH,
+                ).start()
+                return carry
+
+            lax.fori_loop(0, NP // 2, hand, 0)
 
     def send_back(t, block):
         def body(i, carry):
@@ -157,15 +233,23 @@
                 t, pl.ds(pl.multiple_of(dp * POS, POS), POS), pl.ds(pl.multiple_of(dx * TILE, TILE), TILE)
             ]
             mine = jnp.logical_and(dx == x, dp == p)
+            handed = jnp.logical_and(dx == lax.rem(x + 2, 4), lax.rem(dp, 2) == 1)
 
             @pl.when(mine)
             def _():
-                pltpu.make_async_copy(src, back.at[t, head], out_recv.at[t]).start()
-
-            @pl.when(jnp.logical_not(mine))
+                pltpu.make_async_copy(src, place_of(t, head), out_recv.at[t]).start()
+
+            @pl.when(handed)
             def _():
                 pltpu.make_async_remote_copy(
-                    src, back.at[t, head], out_send.at[t], out_recv.at[t],
+                    src, relay_out.at[t, block], out_send.at[t], relay_out_recv.at[t, block],
+                    device_id=device(lax.rem(x + 3 + 2 * lax.rem(x, 2), 4), p), device_id_type=MESH,
+                ).start()
+
+            @pl.when(jnp.logical_not(jnp.logical_or(mine, handed)))
+            def _():
+                pltpu.make_async_remote_copy(
+                    src, place_of(t, head), out_send.at[t], out_recv.at[t],
                     device_id=device(dx, dp), device_id_type=MESH,
                 ).start()
 
@@ -177,15 +261,8 @@
         return pl.ds(pl.multiple_of(i * size, size), size)
 
     def back_here(t):
-        pltpu.make_async_copy(back.at[t], back.at[t], out_recv.at[t]).wait()
-
-    def from_heads(t, store):
-        for c in tiles:
-            for half in range(2):
-                lanes = slice(half * 128, half * 128 + 128)
-                one, two = swap_pair(back[t, 2 * c, :, lanes], back[t, 2 * c + 1, :, lanes], low)
-                store(2 * half, c, one)
-                store(2 * half + 1, c, two)
+        here = back_att if t == AT_ else back.at[t - 1]
+        pltpu.make_async_copy(here, here, out_recv.at[t]).wait()
 
     @pl.when(owner)
     def _():
@@ -249,12 +326,15 @@
 
         lax.fori_loop(0, L // step, query_grad, 0)
 
+    hand_on_out(AT_)
     back_here(AT_)
-
-    def store_att(r, c, tile):
-        att[r, :, c * 128 : c * 128 + 128] = tile
-
-    from_heads(AT_, store_att)
+    for c in tiles:
+        for half in range(2):
+            lanes = slice(half * 128, half * 128 + 128)
+            columns = slice(c * 128, c * 128 + 128)
+            one, two = swap_pair(back_att[2 * c, :, lanes], back_att[2 * c + 1, :, lanes], low)
+            att[2 * half, :, columns] = one
+            att[2 * half + 1, :, columns] = two
     for block in range(3):
         part = lax.dot_general(
             att[...].reshape(ROWS * POS, D),
@@ -290,6 +370,9 @@
 
         lax.fori_loop(0, L // step, key_grad, 0)
 
+    hand_on_out(VG_)
+    hand_on_out(QG_)
+    hand_on_out(KG_)
     pltpu.make_async_copy(w_recv, w_recv, w_recv_sem.at[0]).wait()
     total = w_recv[0].astype(F32)
     for i in range(1, ND):
@@ -310,31 +393,9 @@
         w_mine, w_all.at[pl.ds(pl.multiple_of(me * SLICE, 16), SLICE)], w_recv_sem.at[1]
     ).start()
 
-    def finish(t, result, hbm, sem, masked=False):
+    for t in (VG_, QG_, KG_):
         back_here(t)
-
-        def store(r, c, tile):
-            if masked:
-                tile = jnp.where(spots < lengths[r], tile, jnp.zeros((), BF16))
-            result[r, :, c * 128 : c * 128 + 128] = tile
-
-        from_heads(t, store)
-        copy = pltpu.make_async_copy(result, hbm, store_sem.at[sem])
-        copy.start()
-        return copy
-
-    stores = [
-        finish(VG_, v_in, vg_hbm, 0),
-        finish(QG_, q_in, qg_hbm, 1, masked=True),
-        finish(KG_, k_in, kg_hbm, 2),
-    ]
     pltpu.make_async_copy(w_all, w_all, w_recv_sem.at[1]).wait()
-    for c in range(D // 128):
-        w_out[:, c * 128 : c * 128 + 128] = w_all[c * D : c * D + D, :].astype(F32)
-    stores.append(pltpu.make_async_copy(w_out, wg_hbm, store_sem.at[3]))
-    stores[-1].start()
-    for store in stores:
-        store.wait()
 
     for t in range(4):
         @pl.when(owner)
@@ -348,21 +409,51 @@
         def _():
             pltpu.make_async_copy(stage.at[t], stage.at[t], in_send.at[t]).wait()
 
+        @pl.when(helper_in)
+        def _():
+            pltpu.make_async_copy(relay_in.at[t], relay_in.at[t], relay_send.at[t]).wait()
+
+        @pl.when(helper_out)
+        def _():
+            pltpu.make_async_copy(relay_out.at[t], relay_out.at[t], relay_out_send.at[t]).wait()
+
     for i in range(2):
         sent = w_send.at[pl.ds(0, (ND - 1) * SLICE)]
         pltpu.make_async_copy(sent, sent, w_send_sem.at[i]).wait()
 
 
+def finish(lengths, back, w_all, q_grads, k_grads, v_grads, w_grad):
+    p = lax.axis_index("pos")
+    low = lax.broadcasted_iota(jnp.int32, (POS, 2 * HD), 1) < HD
+    spots = p * POS + lax.broadcasted_iota(jnp.int32, (POS, 2 * HD), 0)
+    for t, result in ((VG_, v_grads), (QG_, q_grads), (KG_, k_grads)):
+        for c in range(2):
+            columns = slice(c * 128, c * 128 + 128)
+            for half in range(2):
+                lanes = slice(half * 128, half * 128 + 128)
+                pair = swap_pair(back[t - 1, 2 * c, :, lanes], back[t - 1, 2 * c + 1, :, lanes], low)
+                for i in range(2):
+                    row, tile = 2 * half + i, pair[i]
+                    if t == QG_:
+                        tile = jnp.where(spots < lengths[row], tile, jnp.zeros((), BF16))
+                    result[row, :, columns] = tile
+    for c in range(2):
+        w_grad[:, c * 128 : c * 128 + 128] = w_all[c * D : c * D + D, :].astype(F32)
+
+
 def per_device(queries, keys, values, out_weight, cotangent, lengths):
     any_space = pl.BlockSpec(memory_space=pl.ANY)
-    local = jax.ShapeDtypeStruct((ROWS, POS, D), BF16)
+    smem = pl.BlockSpec(memory_space=pltpu.SMEM)
     vmem = pltpu.VMEM
     dma = pltpu.SemaphoreType.DMA
-    return pl.pallas_call(
+    back, w_all = pl.pallas_call(
         kernel,
-        out_shape=(local, local, local, jax.ShapeDtypeStruct((D, D), F32)),
-        in_specs=[pl.BlockSpec(memory_space=pltpu.SMEM)] + [any_space] * 5,
-        out_specs=(any_space,) * 4,
+        out_shape=(
+            jax.ShapeDtypeStruct((3, H, POS, TILE), BF16),
+            jax.ShapeDtypeStruct((ND * SLICE, 128), BF16),
+        ),
+        in_specs=[smem] + [any_space] * 5,
+        out_specs=(any_space,) * 2,
         scratch_shapes=[
             vmem((ROWS, POS, D), BF16),
             vmem((ROWS, POS, D), BF16),
@@ -375,14 +466,15 @@
             vmem((L, L), BF16),
             vmem((L, L), BF16),
             vmem((4, L, WIDE), BF16),
-            vmem((4, H, POS, TILE), BF16),
+            vmem((H, POS, TILE), BF16),
             vmem((ROWS, POS, D), BF16),
             vmem((ND * SLICE, 128), BF16),
             vmem((ND, SLICE, 128), BF16),
             vmem((SLICE, 128), BF16),
-            vmem((ND * SLICE, 128), BF16),
-            vmem((D, D), F32),
-            dma((5,)), dma((4,)), dma((4,)), dma((4,)), dma((4,)), dma((2,)), dma((2,)), dma((4,)),
+            vmem((4, 3, POS, TILE), BF16),
+            vmem((4, NP // 2, POS, TILE), BF16),
+            dma((5,)), dma((4,)), dma((4,)), dma((4,)), dma((4,)), dma((2,)), dma((2,)),
+            dma((4,)), dma((4,)), dma((4,)), dma((4, NP // 2)),
         ],
         compiler_params=pltpu.CompilerParams(
             collective_id=0, has_side_effects=True, vmem_limit_bytes=58 * 2**20
@@ -391,6 +483,20 @@
             flops=14 * L**3, bytes_accessed=12 * 2**20, transcendentals=L * L
         ),
     )(lengths, queries, keys, values, cotangent, out_weight)
+    local = jax.ShapeDtypeStruct((ROWS, POS, D), BF16)
+    grads = pl.BlockSpec((ROWS, POS, 256), lambda i: (0, 0, i))
+    return pl.pallas_call(
+        finish,
+        out_shape=(local, local, local, jax.ShapeDtypeStruct((D, D), F32)),
+        grid=(3,),
+        in_specs=[
+            smem,
+            pl.BlockSpec((3, 4, POS, TILE), lambda i: (0, i, 0, 0)),
+            pl.BlockSpec((2 * D, 128), lambda i: (i, 0)),
+        ],
+        out_specs=(grads, grads, grads, pl.BlockSpec((D, 256), lambda i: (0, i))),
+        compiler_params=pltpu.CompilerParams(vmem_limit_bytes=32 * 2**20),
+    )(lengths, back, w_all)
 
 
 def solution(mesh):

time: 154 us -> 150 us (0.974)
  local copies, waits for them, and re-layouts: 6.57 us -> 2.93 us
    unnamed x8 -> x6, local copies, waits for them, and re-layouts: 6.57 us -> 2.93 us
    pallas_call x1 -> x2, Pallas kernels: 145 us -> 145 us  [the longest x1 142 us: per_device(): pl.pallas_call(kernel, out_shape=(jax.ShapeDtypeStruct((3, H, POS, TILE),...]
where the time goes in v2:
time: 150 us; the launch traced here: 149 us
  Pallas kernels  145 us (97%)
  local copies, waits for them, and re-layouts  2.93 us (2%)
    pallas_call x1, Pallas kernels, per_device(): pl.pallas_call(kernel, out_shape=(jax.ShapeDtypeStruct((3, H, POS, TILE),...  142 us
    pallas_call x1, Pallas kernels, per_device(): pl.pallas_call(finish, out_shape=(local, local, local, jax.ShapeDtypeStru...  3.32 us

profile of v2, /device:TPU:16, one launch (start us, length us, event | category | flops | bytes accessed | tf_op | source)
XLA Modules:
  0.0 148.9 jit_solution(12948388799857865335)
XLA Ops:
  0.6 0.0 copy-start.2
  0.6 142.0 %shard_map.93 = (bf16[3,12,128,256]{3,2,1,0:T(8,128)(2,1)}, bf16[4608,128]{1,0:T(8,128)(2,1)}) custom-call(s32[4]{0:T(128)} %lengths.3, bf16[4,128,768]{2,1,0:T(8,128)(2,1)} %q_hbm.1, bf16[4,128,768]{2,1,0:T(8,128)(2,1)} %k_hbm.1, bf16[4,128,768]{2,1,0:T(8,128)(2,1)} %v_hbm.1, bf16[4,128,768]{2,1,0:T(8,128)(2,1)} %c_hbm.1, bf16[768,768]{1,0:T(8,128)(2,1)} %w_hbm.1), custom_call_target="tpu_custom_call" | custom-call | flops 15032385536 | bytes 12582912 | tf_op jit(solution)/shard_map/pallas_call | solution.py:449
  142.6 0.0 copy-done.2
  142.6 0.0 copy-start
  142.6 1.7 %copy-done = bf16[3,12,128,256]{3,2,1,0:T(8,128)(2,1)S(1)} copy-done((bf16[3,12,128,256]{3,2,1,0:T(8,128)(2,1)S(1)}, bf16[3,12,128,256]{3,2,1,0:T(8,128)(2,1)}, u32[]{:S(2)}) %copy-start) | copy-done | bytes 2359320
  144.3 0.0 copy-start.1
  144.3 1.3 copy-done.1
  145.6 3.3 %shard_map.94 = (bf16[4,128,768]{2,1,0:T(8,128)(2,1)}, bf16[4,128,768]{2,1,0:T(8,128)(2,1)}, bf16[4,128,768]{2,1,0:T(8,128)(2,1)}, f32[768,768]{1,0:T(8,128)}) custom-call(s32[4]{0:T(128)S(1)} %copy-done.2, bf16[3,12,128,256]{3,2,1,0:T(8,128)(2,1)S(1)} %copy-done, bf16[4608,128]{1,0:T(8,128)(2,1)S(1)} %copy-done.1), custom_call_target="tpu_custom_call" | custom-call | tf_op jit(solution)/shard_map/pallas_call | solution.py:488
Async XLA Ops:
  0.6 142.0 %copy-start.2 = (s32[4]{0:T(128)S(1)}, s32[4]{0:T(128)}, u32[]{:S(2)}) copy-start(s32[4]{0:T(128)} %lengths.3) | copy-start | bytes 52
  142.6 1.7 %copy-start = (bf16[3,12,128,256]{3,2,1,0:T(8,128)(2,1)S(1)}, bf16[3,12,128,256]{3,2,1,0:T(8,128)(2,1)}, u32[]{:S(2)}) copy-start(bf16[3,12,128,256]{3,2,1,0:T(8,128)(2,1)} %get-tuple-element.6.back) | copy-start | bytes 7077892
  144.3 1.3 copy-start.1

commit v3 on v2

--- a/solution.py
+++ b/solution.py
@@ -19,6 +19,8 @@
 TILE = ROWS * HD
 WIDE = TILE * NX
 SLICE = D * D // 128 // ND
+QUARTER = 8 * SLICE
+HALF = QUARTER // 2
 HEADS_X = H // NX
 MESH = pl.DeviceIdType.MESH
 F32 = jnp.float32
@@ -38,9 +40,9 @@
     lengths, q_hbm, k_hbm, v_hbm, c_hbm, w_hbm,
     back, w_all,
     q_in, k_in, v_in, c_in, w_in, stage, full, probs, probs_b, scores, outs, back_att,
-    att, w_send, w_recv, w_mine, relay_in, relay_out,
-    load_sem, in_send, in_recv, out_send, out_recv, w_send_sem, w_recv_sem,
-    relay_send, relay_recv, relay_out_send, relay_out_recv,
+    att, w_send, w_pass, w_added, w_near, w_mid, w_recv, w_mine, w_quarter, relay_in,
+    load_sem, in_send, in_recv, out_send, out_recv, w_send_sem, w_recv_sem, own_sem,
+    relay_send, relay_recv,
 ):
     x = lax.axis_index("row")
     p = lax.axis_index("pos")
@@ -70,13 +72,6 @@
         hx = lax.rem(oz + 4 - slot, 4)
         h = HEADS_X * hx + lax.rem(2 * slot, 3)
         return h, hx, owner_of(h)[1]
-
-    giver_x = lax.rem(x + 2 * lax.rem(x, 2) + 3, 4)
-    giver_turn = lax.rem(z + 4 - giver_x, 4)
-    giver_k = lax.rem(giver_turn * 2, 3)
-    helper_out = jnp.logical_and(
-        giver_turn < 3, y == lax.rem(giver_k // 2 + core, 2)
-    )
 
     loads = [
         pltpu.make_async_copy(src, dst, load_sem.at[i])
@@ -211,20 +206,6 @@
     def place_of(t, h):
         return back_att.at[h] if t == AT_ else back.at[t - 1, h]
 
-    def hand_on_out(t):
-        @pl.when(helper_out)
-        def _():
-            def hand(block, carry):
-                tile = relay_out.at[t, block]
-                pltpu.make_async_copy(tile, tile, relay_out_recv.at[t, block]).wait()
-                pltpu.make_async_remote_copy(
-                    tile, place_of(t, HEADS_X * giver_x + giver_k), relay_out_send.at[t], out_recv.at[t],
-                    device_id=device(lax.rem(giver_x + 2, 4), 2 * block + 1), device_id_type=MESH,
-                ).start()
-                return carry
-
-            lax.fori_loop(0, NP // 2, hand, 0)
-
     def send_back(t, block):
         def body(i, carry):
             dx = lax.rem(x + lax.rem(i, NX), NX)
@@ -233,20 +214,12 @@
                 t, pl.ds(pl.multiple_of(dp * POS, POS), POS), pl.ds(pl.multiple_of(dx * TILE, TILE), TILE)
             ]
             mine = jnp.logical_and(dx == x, dp == p)
-            handed = jnp.logical_and(dx == lax.rem(x + 2, 4), lax.rem(dp, 2) == 1)
 
             @pl.when(mine)
             def _():
                 pltpu.make_async_copy(src, place_of(t, head), out_recv.at[t]).start()
 
-            @pl.when(handed)
-            def _():
-                pltpu.make_async_remote_copy(
-                    src, relay_out.at[t, block], out_send.at[t], relay_out_recv.at[t, block],
-                    device_id=device(lax.rem(x + 3 + 2 * lax.rem(x, 2), 4), p), device_id_type=MESH,
-                ).start()
-
-            @pl.when(jnp.logical_not(jnp.logical_or(mine, handed)))
+            @pl.when(jnp.logical_not(mine))
             def _():
                 pltpu.make_async_remote_copy(
                     src, place_of(t, head), out_send.at[t], out_recv.at[t],
@@ -326,7 +299,6 @@
 
         lax.fori_loop(0, L // step, query_grad, 0)
 
-    hand_on_out(AT_)
     back_here(AT_)
     for c in tiles:
         for half in range(2):
@@ -344,19 +316,27 @@
         w_send[2 * block * D : 2 * block * D + D, :] = part[:, :128]
         w_send[2 * block * D + D : 2 * block * D + 2 * D, :] = part[:, 128:]
 
-    def scatter(i, carry):
-        other = lax.rem(me + i, ND)
-        pltpu.make_async_remote_copy(
-            w_send.at[pl.ds(pl.multiple_of(other * SLICE, 16), SLICE)], w_recv.at[me],
-            w_send_sem.at[0], w_recv_sem.at[0],
-            device_id=device(other // NP, lax.rem(other, NP)), device_id_type=MESH,
-        ).start()
-        return carry
-
-    lax.fori_loop(1, ND, scatter, 0)
-    pltpu.make_async_copy(
-        w_send.at[pl.ds(pl.multiple_of(me * SLICE, 16), SLICE)], w_recv.at[me], w_recv_sem.at[0]
-    ).start()
+    ahead, behind = lax.rem(z + 1, 4), lax.rem(z + 3, 4)
+    opposite = lax.rem(z + 2, 4)
+
+    def along_z(src, dst, to, sent, got):
+        return pltpu.make_async_remote_copy(
+            src, dst, w_send_sem.at[sent], w_recv_sem.at[got],
+            device_id=device(x, y * 4 + to), device_id_type=MESH,
+        )
+
+    def part_of(ref, quarter, half=None):
+        if half is None:
+            return ref.at[pl.ds(pl.multiple_of(quarter * QUARTER, 16), QUARTER)]
+        return ref.at[pl.ds(pl.multiple_of(quarter * QUARTER + half * HALF, 16), HALF)]
+
+    def half_of(ref, half):
+        return ref.at[pl.ds(half * HALF, HALF)]
+
+    along_z(part_of(w_send, opposite, 0), w_pass.at[0], ahead, 0, 0).start()
+    along_z(part_of(w_send, opposite, 1), w_pass.at[1], behind, 0, 1).start()
+    along_z(part_of(w_send, ahead, 1), half_of(w_near.at[0], 1), ahead, 1, 2).start()
+    along_z(part_of(w_send, behind, 0), half_of(w_near.at[1], 0), behind, 1, 2).start()
 
     @pl.when(owner)
     def _():
@@ -370,32 +350,56 @@
 
         lax.fori_loop(0, L // step, key_grad, 0)
 
-    hand_on_out(VG_)
-    hand_on_out(QG_)
-    hand_on_out(KG_)
-    pltpu.make_async_copy(w_recv, w_recv, w_recv_sem.at[0]).wait()
+    for i, to in ((0, ahead), (1, behind)):
+        pltpu.make_async_copy(w_pass.at[i], w_pass.at[i], w_recv_sem.at[i]).wait()
+        rows = pl.ds(pl.multiple_of(to * QUARTER + i * HALF, 16), HALF)
+        w_added[i] = (w_pass[i].astype(F32) + w_send[rows, :].astype(F32)).astype(BF16)
+        along_z(w_added.at[i], half_of(w_near.at[i], i), to, 1, 2).start()
+    pltpu.make_async_copy(w_near, w_near, w_recv_sem.at[2]).wait()
+    rows = pl.ds(pl.multiple_of(z * QUARTER, 16), QUARTER)
+    w_mid[...] = (
+        w_near[0].astype(F32) + w_near[1].astype(F32) + w_send[rows, :].astype(F32)
+    ).astype(BF16)
+
+    spot = x * 2 + y
+
+    def across(src_of, dst, sem, got):
+        def body(i, carry):
+            other = lax.rem(spot + i, 8)
+            pltpu.make_async_remote_copy(
+                src_of(other), dst, w_send_sem.at[sem], w_recv_sem.at[got],
+                device_id=device(other // 2, lax.rem(other, 2) * 4 + z), device_id_type=MESH,
+            ).start()
+            return carry
+
+        lax.fori_loop(1, 8, body, 0)
+        pltpu.make_async_copy(src_of(spot), dst, w_recv_sem.at[got]).start()
+
+    def slice_of(ref, i):
+        return ref.at[pl.ds(pl.multiple_of(i * SLICE, 16), SLICE)]
+
+    across(lambda i: slice_of(w_mid, i), w_recv.at[spot], 2, 3)
+    pltpu.make_async_copy(w_recv, w_recv, w_recv_sem.at[3]).wait()
     total = w_recv[0].astype(F32)
-    for i in range(1, ND):
+    for i in range(1, 8):
         total = total + w_recv[i].astype(F32)
     w_mine[...] = total.astype(BF16)
-
-    def spread(i, carry):
-        other = lax.rem(me + i, ND)
-        pltpu.make_async_remote_copy(
-            w_mine, w_all.at[pl.ds(pl.multiple_of(me * SLICE, 16), SLICE)],
-            w_send_sem.at[1], w_recv_sem.at[1],
-            device_id=device(other // NP, lax.rem(other, NP)), device_id_type=MESH,
-        ).start()
-        return carry
-
-    lax.fori_loop(1, ND, spread, 0)
-    pltpu.make_async_copy(
-        w_mine, w_all.at[pl.ds(pl.multiple_of(me * SLICE, 16), SLICE)], w_recv_sem.at[1]
-    ).start()
+    across(lambda i: w_mine, slice_of(w_quarter, spot), 3, 4)
+    pltpu.make_async_copy(w_quarter, w_quarter, w_recv_sem.at[4]).wait()
+    along_z(w_quarter, part_of(w_all, z), ahead, 4, 5).start()
+    along_z(w_quarter, part_of(w_all, z), behind, 4, 6).start()
+    own_copy = pltpu.make_async_copy(w_quarter, part_of(w_all, z), own_sem.at[0])
+    own_copy.start()
+    for i, (came, to) in enumerate(((behind, ahead), (ahead, behind))):
+        here = part_of(w_all, came)
+        pltpu.make_async_copy(here, here, w_recv_sem.at[5 + i]).wait()
+        along_z(part_of(w_all, came, i), part_of(w_all, came, i), to, 5, 7).start()
 
     for t in (VG_, QG_, KG_):
         back_here(t)
-    pltpu.make_async_copy(w_all, w_all, w_recv_sem.at[1]).wait()
+    here = part_of(w_all, opposite)
+    pltpu.make_async_copy(here, here, w_recv_sem.at[7]).wait()
+    own_copy.wait()
 
     for t in range(4):
         @pl.when(owner)
@@ -413,13 +417,11 @@
         def _():
             pltpu.make_async_copy(relay_in.at[t], relay_in.at[t], relay_send.at[t]).wait()
 
-        @pl.when(helper_out)
-        def _():
-            pltpu.make_async_copy(relay_out.at[t], relay_out.at[t], relay_out_send.at[t]).wait()
-
-    for i in range(2):
-        sent = w_send.at[pl.ds(0, (ND - 1) * SLICE)]
-        pltpu.make_async_copy(sent, sent, w_send_sem.at[i]).wait()
+    for sem, sent in (
+        (0, w_pass), (1, w_near), (2, w_recv.at[pl.ds(0, 7)]), (3, w_recv.at[pl.ds(0, 7)]),
+        (4, w_near), (5, w_pass),
+    ):
+        pltpu.make_async_copy(sent, sent, w_send_sem.at[sem]).wait()
 
 
 def finish(lengths, back, w_all, q_grads, k_grads, v_grads, w_grad):
@@ -427,18 +429,15 @@
     low = lax.broadcasted_iota(jnp.int32, (POS, 2 * HD), 1) < HD
     spots = p * POS + lax.broadcasted_iota(jnp.int32, (POS, 2 * HD), 0)
     for t, result in ((VG_, v_grads), (QG_, q_grads), (KG_, k_grads)):
-        for c in range(2):
-            columns = slice(c * 128, c * 128 + 128)
-            for half in range(2):
-                lanes = slice(half * 128, half * 128 + 128)
-                pair = swap_pair(back[t - 1, 2 * c, :, lanes], back[t - 1, 2 * c + 1, :, lanes], low)
-                for i in range(2):
-                    row, tile = 2 * half + i, pair[i]
-                    if t == QG_:
-                        tile = jnp.where(spots < lengths[row], tile, jnp.zeros((), BF16))
-                    result[row, :, columns] = tile
-    for c in range(2):
-        w_grad[:, c * 128 : c * 128 + 128] = w_all[c * D : c * D + D, :].astype(F32)
+        for half in range(2):
+            lanes = slice(half * 128, half * 128 + 128)
+            pair = swap_pair(back[t - 1, 0, :, lanes], back[t - 1, 1, :, lanes], low)
+            for i in range(2):
+                row, tile = 2 * half + i, pair[i]
+                if t == QG_:
+                    tile = jnp.where(spots < lengths[row], tile, jnp.zeros((), BF16))
+                result[row] = tile
+    w_grad[...] = w_all[...].astype(F32)
 
 
 def per_device(queries, keys, values, out_weight, cotangent, lengths):
@@ -469,12 +468,16 @@
             vmem((H, POS, TILE), BF16),
             vmem((ROWS, POS, D), BF16),
             vmem((ND * SLICE, 128), BF16),
-            vmem((ND, SLICE, 128), BF16),
+            vmem((2, HALF, 128), BF16),
+            vmem((2, HALF, 128), BF16),
+            vmem((2, QUARTER, 128), BF16),
+            vmem((QUARTER, 128), BF16),
+            vmem((8, SLICE, 128), BF16),
             vmem((SLICE, 128), BF16),
+            vmem((QUARTER, 128), BF16),
             vmem((4, 3, POS, TILE), BF16),
-            vmem((4, NP // 2, POS, TILE), BF16),
-            dma((5,)), dma((4,)), dma((4,)), dma((4,)), dma((4,)), dma((2,)), dma((2,)),
-            dma((4,)), dma((4,)), dma((4,)), dma((4, NP // 2)),
+            dma((5,)), dma((4,)), dma((4,)), dma((4,)), dma((4,)), dma((6,)), dma((8,)), dma((1,)),
+            dma((4,)), dma((4,)),
         ],
         compiler_params=pltpu.CompilerParams(
             collective_id=0, has_side_effects=True, vmem_limit_bytes=58 * 2**20
@@ -484,18 +487,18 @@
         ),
     )(lengths, queries, keys, values, cotangent, out_weight)
     local = jax.ShapeDtypeStruct((ROWS, POS, D), BF16)
-    grads = pl.BlockSpec((ROWS, POS, 256), lambda i: (0, 0, i))
+    grads = pl.BlockSpec((ROWS, POS, 128), lambda i: (0, 0, i))
     return pl.pallas_call(
         finish,
         out_shape=(local, local, local, jax.ShapeDtypeStruct((D, D), F32)),
-        grid=(3,),
+        grid=(H // 2,),
         in_specs=[
             smem,
-            pl.BlockSpec((3, 4, POS, TILE), lambda i: (0, i, 0, 0)),
-            pl.BlockSpec((2 * D, 128), lambda i: (i, 0)),
+            pl.BlockSpec((3, 2, POS, TILE), lambda i: (0, i, 0, 0)),
+            pl.BlockSpec((D, 128), lambda i: (i, 0)),
         ],
-        out_specs=(grads, grads, grads, pl.BlockSpec((D, 256), lambda i: (0, i))),
-        compiler_params=pltpu.CompilerParams(vmem_limit_bytes=32 * 2**20),
+        out_specs=(grads, grads, grads, pl.BlockSpec((D, 128), lambda i: (0, i))),
+        compiler_params=pltpu.CompilerParams(vmem_limit_bytes=60 * 2**20),
     )(lengths, back, w_all)
 
 

time: 150 us -> 148 us (0.987)
  local copies, waits for them, and re-layouts: 2.93 us -> 0 us
  Pallas kernels: 145 us -> 147 us
    unnamed x6 -> x0, local copies, waits for them, and re-layouts: 2.93 us -> none
    pallas_call x1, Pallas kernels: 3.32 us -> 6.02 us  [per_device(): pl.pallas_call(finish, out_shape=(local, local, local, jax.ShapeDtypeStru...]
where the time goes in v3:
time: 148 us
  Pallas kernels  147 us (99%)
    pallas_call x1, Pallas kernels, per_device(): pl.pallas_call(kernel, out_shape=(jax.ShapeDtypeStruct((3, H, POS, TILE),...  141 us
    pallas_call x1, Pallas kernels, per_device(): pl.pallas_call(finish, out_shape=(local, local, local, jax.ShapeDtypeStru...  6.02 us

profile of v3, /device:TPU:16, one launch (start us, length us, event | category | flops | bytes accessed | tf_op | source)
XLA Modules:
  0.0 147.6 jit_solution(1722582792587178703)
XLA Ops:
  0.6 140.9 %shard_map.93 = (bf16[3,12,128,256]{3,2,1,0:T(8,128)(2,1)}, bf16[4608,128]{1,0:T(8,128)(2,1)}) custom-call(s32[4]{0:T(128)} %lengths.3, bf16[4,128,768]{2,1,0:T(8,128)(2,1)} %q_hbm.1, bf16[4,128,768]{2,1,0:T(8,128)(2,1)} %k_hbm.1, bf16[4,128,768]{2,1,0:T(8,128)(2,1)} %v_hbm.1, bf16[4,128,768]{2,1,0:T(8,128)(2,1)} %c_hbm.1, bf16[768,768]{1,0:T(8,128)(2,1)} %w_hbm.1), custom_call_target="tpu_custom_call" | custom-call | flops 15032385536 | bytes 12582912 | tf_op jit(solution)/shard_map/pallas_call | solution.py:448
  141.5 6.0 %shard_map.94 = (bf16[4,128,768]{2,1,0:T(8,128)(2,1)}, bf16[4,128,768]{2,1,0:T(8,128)(2,1)}, bf16[4,128,768]{2,1,0:T(8,128)(2,1)}, f32[768,768]{1,0:T(8,128)}) custom-call(s32[4]{0:T(128)} %lengths.3, bf16[3,12,128,256]{3,2,1,0:T(8,128)(2,1)} %get-tuple-element.6.back, bf16[4608,128]{1,0:T(8,128)(2,1)} %get-tuple-element.7.w_all), custom_call_target="tpu_custom_call" | custom-call | tf_op jit(solution)/shard_map/pallas_call | solution.py:491

commit v4 on v3

--- a/solution.py
+++ b/solution.py
@@ -19,8 +19,8 @@
 TILE = ROWS * HD
 WIDE = TILE * NX
 SLICE = D * D // 128 // ND
-QUARTER = 8 * SLICE
-HALF = QUARTER // 2
+SHARES = (80, 64)
+BASES = (0, ND * SHARES[0])
 HEADS_X = H // NX
 MESH = pl.DeviceIdType.MESH
 F32 = jnp.float32
@@ -40,10 +40,13 @@
     lengths, q_hbm, k_hbm, v_hbm, c_hbm, w_hbm,
     back, w_all,
     q_in, k_in, v_in, c_in, w_in, stage, full, probs, probs_b, scores, outs, back_att,
-    att, w_send, w_pass, w_added, w_near, w_mid, w_recv, w_mine, w_quarter, relay_in,
+    att, w_send, w_first_a, w_first_b, w_mid_a, w_mid_b, w_second_a, w_second_b,
+    w_quarter_a, w_quarter_b, relay_in,
     load_sem, in_send, in_recv, out_send, out_recv, w_send_sem, w_recv_sem, own_sem,
     relay_send, relay_recv,
 ):
+    w_first, w_mid = (w_first_a, w_first_b), (w_mid_a, w_mid_b)
+    w_second, w_quarter = (w_second_a, w_second_b), (w_quarter_a, w_quarter_b)
     x = lax.axis_index("row")
     p = lax.axis_index("pos")
     core = lax.rem(lax.axis_index("batch"), 2)
@@ -277,28 +280,6 @@
 
         lax.fori_loop(0, L // step, value_grad, 0)
 
-        def score_grad(i, carry):
-            rows = rows_at(i, POS)
-            grads = lax.dot_general(
-                full[A_, rows, :], full[V_], (((1,), (1,)), ((), ())), preferred_element_type=F32
-            )
-            prob = probs[rows, :]
-            centre = jnp.sum(prob * grads, axis=-1, keepdims=True)
-            scores[rows, :] = (scale * prob * (grads - centre)).astype(BF16)
-            return carry
-
-        lax.fori_loop(0, L // POS, score_grad, 0)
-
-        def query_grad(i, carry):
-            rows = rows_at(i)
-            outs[QG_, rows, :] = jnp.dot(
-                scores[rows, :], full[K_], preferred_element_type=F32
-            ).astype(BF16)
-            send_back(QG_, i)
-            return carry
-
-        lax.fori_loop(0, L // step, query_grad, 0)
-
     back_here(AT_)
     for c in tiles:
         for half in range(2):
@@ -316,27 +297,77 @@
         w_send[2 * block * D : 2 * block * D + D, :] = part[:, :128]
         w_send[2 * block * D + D : 2 * block * D + 2 * D, :] = part[:, 128:]
 
-    ahead, behind = lax.rem(z + 1, 4), lax.rem(z + 3, 4)
-    opposite = lax.rem(z + 2, 4)
-
-    def along_z(src, dst, to, sent, got):
-        return pltpu.make_async_remote_copy(
-            src, dst, w_send_sem.at[sent], w_recv_sem.at[got],
-            device_id=device(x, y * 4 + to), device_id_type=MESH,
-        )
-
-    def part_of(ref, quarter, half=None):
-        if half is None:
-            return ref.at[pl.ds(pl.multiple_of(quarter * QUARTER, 16), QUARTER)]
-        return ref.at[pl.ds(pl.multiple_of(quarter * QUARTER + half * HALF, 16), HALF)]
-
-    def half_of(ref, half):
-        return ref.at[pl.ds(half * HALF, HALF)]
-
-    along_z(part_of(w_send, opposite, 0), w_pass.at[0], ahead, 0, 0).start()
-    along_z(part_of(w_send, opposite, 1), w_pass.at[1], behind, 0, 1).start()
-    along_z(part_of(w_send, ahead, 1), half_of(w_near.at[0], 1), ahead, 1, 2).start()
-    along_z(part_of(w_send, behind, 0), half_of(w_near.at[1], 0), behind, 1, 2).start()
+    places = (z, x)
+    spots_of = (x * 2 + y, z * 2 + y)
+
+    def on_ring(part, other):
+        return device(x, y * 4 + other) if part == 0 else device(other, p)
+
+    def on_face(part, other):
+        side = lax.rem(other, 2) * 4
+        return device(other // 2, side + z) if part == 0 else device(x, side + other // 2)
+
+    def rows_of(part, index, step):
+        return pl.ds(pl.multiple_of(BASES[part] + index * step, 16), step)
+
+    def share(part, count=8):
+        return count * SHARES[part]
+
+    def send(src, dst, sems, part, to):
+        pltpu.make_async_remote_copy(
+            src, dst, w_send_sem.at[sems, part], w_recv_sem.at[sems, part],
+            device_id=to, device_id_type=MESH,
+        ).start()
+
+    def took(ref, sems, part):
+        pltpu.make_async_copy(ref, ref, w_recv_sem.at[sems, part]).wait()
+
+    for part in range(2):
+        for i in range(1, 4):
+            other = lax.rem(places[part] + i, 4)
+            send(
+                w_send.at[rows_of(part, other, share(part))], w_first[part].at[i - 1],
+                0, part, on_ring(part, other),
+            )
+
+    @pl.when(owner)
+    def _():
+        def score_grad(i, carry):
+            rows = rows_at(i, POS)
+            grads = lax.dot_general(
+                full[A_, rows, :], full[V_], (((1,), (1,)), ((), ())), preferred_element_type=F32
+            )
+            prob = probs[rows, :]
+            centre = jnp.sum(prob * grads, axis=-1, keepdims=True)
+            scores[rows, :] = (scale * prob * (grads - centre)).astype(BF16)
+            return carry
+
+        lax.fori_loop(0, L // POS, score_grad, 0)
+
+        def query_grad(i, carry):
+            rows = rows_at(i)
+            outs[QG_, rows, :] = jnp.dot(
+                scores[rows, :], full[K_], preferred_element_type=F32
+            ).astype(BF16)
+            send_back(QG_, i)
+            return carry
+
+        lax.fori_loop(0, L // step, query_grad, 0)
+
+    for part in range(2):
+        took(w_first[part], 0, part)
+        own = w_send[rows_of(part, places[part], share(part)), :].astype(F32)
+        w_mid[part][...] = (
+            (own + w_first[part][0].astype(F32))
+            + (w_first[part][1].astype(F32) + w_first[part][2].astype(F32))
+        ).astype(BF16)
+        for i in range(1, 8):
+            other = lax.rem(spots_of[part] + i, 8)
+            start = pl.multiple_of(other * SHARES[part], 16)
+            send(
+                w_mid[part].at[pl.ds(start, SHARES[part])], w_second[part].at[i - 1],
+                1, part, on_face(part, other),
+            )
 
     @pl.when(owner)
     def _():
@@ -350,56 +381,33 @@
 
         lax.fori_loop(0, L // step, key_grad, 0)
 
-    for i, to in ((0, ahead), (1, behind)):
-        pltpu.make_async_copy(w_pass.at[i], w_pass.at[i], w_recv_sem.at[i]).wait()
-        rows = pl.ds(pl.multiple_of(to * QUARTER + i * HALF, 16), HALF)
-        w_added[i] = (w_pass[i].astype(F32) + w_send[rows, :].astype(F32)).astype(BF16)
-        along_z(w_added.at[i], half_of(w_near.at[i], i), to, 1, 2).start()
-    pltpu.make_async_copy(w_near, w_near, w_recv_sem.at[2]).wait()
-    rows = pl.ds(pl.multiple_of(z * QUARTER, 16), QUARTER)
-    w_mid[...] = (
-        w_near[0].astype(F32) + w_near[1].astype(F32) + w_send[rows, :].astype(F32)
-    ).astype(BF16)
-
-    spot = x * 2 + y
-
-    def across(src_of, dst, sem, got):
-        def body(i, carry):
-            other = lax.rem(spot + i, 8)
-            pltpu.make_async_remote_copy(
-                src_of(other), dst, w_send_sem.at[sem], w_recv_sem.at[got],
-                device_id=device(other // 2, lax.rem(other, 2) * 4 + z), device_id_type=MESH,
-            ).start()
-            return carry
-
-        lax.fori_loop(1, 8, body, 0)
-        pltpu.make_async_copy(src_of(spot), dst, w_recv_sem.at[got]).start()
-
-    def slice_of(ref, i):
-        return ref.at[pl.ds(pl.multiple_of(i * SLICE, 16), SLICE)]
-
-    across(lambda i: slice_of(w_mid, i), w_recv.at[spot], 2, 3)
-    pltpu.make_async_copy(w_recv, w_recv, w_recv_sem.at[3]).wait()
-    total = w_recv[0].astype(F32)
-    for i in range(1, 8):
-        total = total + w_recv[i].astype(F32)
-    w_mine[...] = total.astype(BF16)
-    across(lambda i: w_mine, slice_of(w_quarter, spot), 3, 4)
-    pltpu.make_async_copy(w_quarter, w_quarter, w_recv_sem.at[4]).wait()
-    along_z(w_quarter, part_of(w_all, z), ahead, 4, 5).start()
-    along_z(w_quarter, part_of(w_all, z), behind, 4, 6).start()
-    own_copy = pltpu.make_async_copy(w_quarter, part_of(w_all, z), own_sem.at[0])
-    own_copy.start()
-    for i, (came, to) in enumerate(((behind, ahead), (ahead, behind))):
-        here = part_of(w_all, came)
-        pltpu.make_async_copy(here, here, w_recv_sem.at[5 + i]).wait()
-        along_z(part_of(w_all, came, i), part_of(w_all, came, i), to, 5, 7).start()
+    for part in range(2):
+        took(w_second[part], 1, part)
+        here = pl.ds(pl.multiple_of(spots_of[part] * SHARES[part], 16), SHARES[part])
+        total = w_mid[part][here, :].astype(F32)
+        for i in range(7):
+            total = total + w_second[part][i].astype(F32)
+        w_quarter[part][here, :] = total.astype(BF16)
+        for i in range(1, 8):
+            other = lax.rem(spots_of[part] + i, 8)
+            send(
+                w_quarter[part].at[here], w_quarter[part].at[here], 2, part, on_face(part, other)
+            )
+    own_copies = []
+    for part in range(2):
+        took(w_quarter[part].at[pl.ds(0, share(part, 7))], 2, part)
+        there = w_all.at[rows_of(part, places[part], share(part))]
+        for i in range(1, 4):
+            other = lax.rem(places[part] + i, 4)
+            send(w_quarter[part], there, 3, part, on_ring(part, other))
+        own_copies.append(pltpu.make_async_copy(w_quarter[part], there, own_sem.at[part]))
+        own_copies[-1].start()
 
     for t in (VG_, QG_, KG_):
         back_here(t)
-    here = part_of(w_all, opposite)
-    pltpu.make_async_copy(here, here, w_recv_sem.at[7]).wait()
-    own_copy.wait()
+    for part in range(2):
+        took(w_all.at[pl.ds(BASES[part], share(part, 24))], 3, part)
+        own_copies[part].wait()
 
     for t in range(4):
         @pl.when(owner)
@@ -417,11 +425,10 @@
         def _():
             pltpu.make_async_copy(relay_in.at[t], relay_in.at[t], relay_send.at[t]).wait()
 
-    for sem, sent in (
-        (0, w_pass), (1, w_near), (2, w_recv.at[pl.ds(0, 7)]), (3, w_recv.at[pl.ds(0, 7)]),
-        (4, w_near), (5, w_pass),
-    ):
-        pltpu.make_async_copy(sent, sent, w_send_sem.at[sem]).wait()
+    for part in range(2):
+        for sems, rows in enumerate((24, 7, 7, 24)):
+            sent = w_send.at[pl.ds(0, share(part, rows))]
+            pltpu.make_async_copy(sent, sent, w_send_sem.at[sems, part]).wait()
 
 
 def finish(lengths, back, w_all, q_grads, k_grads, v_grads, w_grad):
@@ -468,15 +475,12 @@
             vmem((H, POS, TILE), BF16),
             vmem((ROWS, POS, D), BF16),
             vmem((ND * SLICE, 128), BF16),
-            vmem((2, HALF, 128), BF16),
-            vmem((2, HALF, 128), BF16),
-            vmem((2, QUARTER, 128), BF16),
-            vmem((QUARTER, 128), BF16),
-            vmem((8, SLICE, 128), BF16),
-            vmem((SLICE, 128), BF16),
-            vmem((QUARTER, 128), BF16),
+            *(vmem((3, 8 * share, 128), BF16) for share in SHARES),
+            *(vmem((8 * share, 128), BF16) for share in SHARES),
+            *(vmem((7, share, 128), BF16) for share in SHARES),
+            *(vmem((8 * share, 128), BF16) for share in SHARES),
             vmem((4, 3, POS, TILE), BF16),
-            dma((5,)), dma((4,)), dma((4,)), dma((4,)), dma((4,)), dma((6,)), dma((8,)), dma((1,)),
+            dma((5,)), dma((4,)), dma((4,)), dma((4,)), dma((4,)), dma((4, 2)), dma((4, 2)), dma((2,)),
             dma((4,)), dma((4,)),
         ],
         compiler_params=pltpu.CompilerParams(

time: 148 us -> 140 us (0.946)
  the two profiles are of different devices: /device:TPU:16 before, /device:TPU:28 now
where the time goes in v4:
time: 140 us; the launch traced here: 139 us
  Pallas kernels  139 us (99%)
    pallas_call x1, Pallas kernels, per_device(): pl.pallas_call(kernel, out_shape=(jax.ShapeDtypeStruct((3, H, POS, TILE),...  133 us
    pallas_call x1, Pallas kernels, per_device(): pl.pallas_call(finish, out_shape=(local, local, local, jax.ShapeDtypeStru...  6.02 us

profile of v4, /device:TPU:28, one launch (start us, length us, event | category | flops | bytes accessed | tf_op | source)
XLA Modules:
  0.0 139.5 jit_solution(18061038850914786343)
XLA Ops:
  0.6 132.8 %shard_map.93 = (bf16[3,12,128,256]{3,2,1,0:T(8,128)(2,1)}, bf16[4608,128]{1,0:T(8,128)(2,1)}) custom-call(s32[4]{0:T(128)} %lengths.3, bf16[4,128,768]{2,1,0:T(8,128)(2,1)} %q_hbm.1, bf16[4,128,768]{2,1,0:T(8,128)(2,1)} %k_hbm.1, bf16[4,128,768]{2,1,0:T(8,128)(2,1)} %v_hbm.1, bf16[4,128,768]{2,1,0:T(8,128)(2,1)} %c_hbm.1, bf16[768,768]{1,0:T(8,128)(2,1)} %w_hbm.1), custom_call_target="tpu_custom_call" | custom-call | flops 15032385536 | bytes 12582912 | tf_op jit(solution)/shard_map/pallas_call | solution.py:455
  133.4 6.0 %shard_map.94 = (bf16[4,128,768]{2,1,0:T(8,128)(2,1)}, bf16[4,128,768]{2,1,0:T(8,128)(2,1)}, bf16[4,128,768]{2,1,0:T(8,128)(2,1)}, f32[768,768]{1,0:T(8,128)}) custom-call(s32[4]{0:T(128)} %lengths.3, bf16[3,12,128,256]{3,2,1,0:T(8,128)(2,1)} %get-tuple-element.6.back, bf16[4608,128]{1,0:T(8,128)(2,1)} %get-tuple-element.7.w_all), custom_call_target="tpu_custom_call" | custom-call | tf_op jit(solution)/shard_map/pallas_call | solution.py:495

commit v5 on v1

v5 whole, which is shorter than its diff:
```python
import math

import jax
import jax.numpy as jnp
from jax import lax
from jax.experimental import pallas as pl
from jax.experimental.pallas import tpu as pltpu
from jax.sharding import PartitionSpec as P

H = 12
HD = 64
D = 768
ROWS = 4
POS = 128
NX = 4
NP = 8
ND = NX * NP
L = POS * NP
TILE = ROWS * HD
WIDE = TILE * NX
SLICE = D * D // 128 // ND
SHARES = (80, 64)
BASES = (0, ND * SHARES[0])
HEADS_X = H // NX
MESH = pl.DeviceIdType.MESH
F32 = jnp.float32
BF16 = jnp.bfloat16

K_, Q_, V_, A_ = range(4)
AT_, VG_, QG_, KG_ = range(4)


def swap_pair(first, second, low):
    first_r = jnp.concatenate([first[:, HD:], first[:, :HD]], axis=1)
    second_r = jnp.concatenate([second[:, HD:], second[:, :HD]], axis=1)
    return jnp.where(low, first, second_r), jnp.where(low, first_r, second)


def kernel(
    lengths, q_hbm, k_hbm, v_hbm, c_hbm, w_hbm,
    back, w_all,
    q_in, k_in, v_in, c_in, w_in, stage, full, probs, probs_b, scores, outs, back_att,
    att, w_send, w_first_a, w_first_b, w_mid_a, w_mid_b, w_second_a, w_second_b,
    w_block_a, w_block_b,
    load_sem, in_send, in_recv, out_send, out_recv, w_send_sem, w_recv_sem, own_sem,
):
    w_first, w_mid = (w_first_a, w_first_b), (w_mid_a, w_mid_b)
    w_second, w_block = (w_second_a, w_second_b), (w_block_a, w_block_b)
    x = lax.axis_index("row")
    p = lax.axis_index("pos")
    core = lax.rem(lax.axis_index("batch"), 2)
    me = x * NP + p
    turn = lax.rem(lax.rem(p, 4) + 4 - x, 4)
    own_k = lax.rem(turn * 2, 3)
    owner = jnp.logical_and(turn < 3, p // 4 == lax.rem(own_k // 2 + core, 2))
    head = HEADS_X * x + own_k

    def owner_of(h):
        hx, hk = h // HEADS_X, lax.rem(h, HEADS_X)
        return hx, lax.rem(hk // 2 + core, 2) * 4 + lax.rem(lax.rem(2 * hk, 3) + hx, 4)

    def device(dx, dp):
        return {"row": dx, "pos": dp}

    y, z = p // 4, lax.rem(p, 4)

    loads = [
        pltpu.make_async_copy(src, dst, load_sem.at[i])
        for i, (src, dst) in enumerate(
            ((k_hbm, k_in), (q_hbm, q_in), (v_hbm, v_in), (c_hbm, c_in), (w_hbm, w_in))
        )
    ]
    for load in loads:
        load.start()

    barrier = pltpu.get_barrier_semaphore()

    def greet(i, carry):
        other = lax.rem(me + i, ND)
        pl.semaphore_signal(
            barrier, inc=1, device_id=device(other // NP, lax.rem(other, NP)), device_id_type=MESH
        )
        return carry

    @pl.when(owner)
    def _():
        lax.fori_loop(1, ND, greet, 0)


    low = lax.broadcasted_iota(jnp.int32, (POS, 2 * HD), 1) < HD
    spots = p * POS + lax.broadcasted_iota(jnp.int32, (POS, 2 * HD), 0)

    def to_heads(t, rows_of, tiles):
        for c in tiles:
            for half in range(2):
                even, odd = swap_pair(rows_of(2 * half, c), rows_of(2 * half + 1, c), low)
                lanes = slice(half * 128, half * 128 + 128)
                stage[t, 2 * c, :, lanes] = even
                stage[t, 2 * c + 1, :, lanes] = odd

    def send_heads(t):
        def body(i, carry):
            h = lax.rem(i + HEADS_X * x, H)
            hx, hp = owner_of(h)
            place = full.at[
                t, pl.ds(pl.multiple_of(p * POS, POS), POS), pl.ds(pl.multiple_of(x * TILE, TILE), TILE)
            ]
            mine = jnp.logical_and(hx == x, hp == p)

            @pl.when(mine)
            def _():
                pltpu.make_async_copy(stage.at[t, h], place, in_recv.at[t]).start()

            @pl.when(jnp.logical_not(mine))
            def _():
                pltpu.make_async_remote_copy(
                    stage.at[t, h], place, in_send.at[t], in_recv.at[t],
                    device_id=device(hx, hp), device_id_type=MESH,
                ).start()

            return carry

        lax.fori_loop(0, H, body, 0)

    tiles = range(H // 2)
    loads[0].wait()
    to_heads(K_, lambda r, c: k_in[r, :, c * 128 : c * 128 + 128], tiles)
    pl.semaphore_wait(barrier, H - owner.astype(jnp.int32))
    send_heads(K_)
    loads[1].wait()
    to_heads(
        Q_,
        lambda r, c: jnp.where(
            spots < lengths[r], q_in[r, :, c * 128 : c * 128 + 128], jnp.zeros((), BF16)
        ),
        tiles,
    )
    send_heads(Q_)
    loads[2].wait()
    to_heads(V_, lambda r, c: v_in[r, :, c * 128 : c * 128 + 128], tiles)
    send_heads(V_)
    loads[3].wait()
    loads[4].wait()
    for block in range(3):
        part = lax.dot_general(
            c_in[...].reshape(ROWS * POS, D), w_in[block * 256 : block * 256 + 256, :],
            (((1,), (1,)), ((), ())), preferred_element_type=F32,
        ).astype(BF16)
        to_heads(
            A_,
            lambda r, c: part[r * POS : r * POS + POS, (c - 2 * block) * 128 : (c - 2 * block) * 128 + 128],
            (2 * block, 2 * block + 1),
        )
    send_heads(A_)

    scale = 1.0 / math.sqrt(HD * ROWS * NX)
    step = 256

    def arrived(t):
        pltpu.make_async_copy(full.at[t], full.at[t], in_recv.at[t]).wait()

    def place_of(t, h):
        return back_att.at[h] if t == AT_ else back.at[t - 1, h]

    def send_back(t, block):
        def body(i, carry):
            dx = lax.rem(x + lax.rem(i, NX), NX)
            dp = block * 2 + i // NX
            src = outs.at[
                t, pl.ds(pl.multiple_of(dp * POS, POS), POS), pl.ds(pl.multiple_of(dx * TILE, TILE), TILE)
            ]
            mine = jnp.logical_and(dx == x, dp == p)

            @pl.when(mine)
            def _():
                pltpu.make_async_copy(src, place_of(t, head), out_recv.at[t]).start()

            @pl.when(jnp.logical_not(mine))
            def _():
                pltpu.make_async_remote_copy(
                    src, place_of(t, head), out_send.at[t], out_recv.at[t],
                    device_id=device(dx, dp), device_id_type=MESH,
                ).start()

            return carry

        lax.fori_loop(0, 2 * NX, body, 0)

    def rows_at(i, size=step):
        return pl.ds(pl.multiple_of(i * size, size), size)

    def back_here(t):
        here = back_att if t == AT_ else back.at[t - 1]
        pltpu.make_async_copy(here, here, out_recv.at[t]).wait()

    def as_owner(work):
        pl.when(owner)(work)

    def softmax():
        arrived(K_)
        arrived(Q_)

        def body(i, carry):
            rows = rows_at(i, 2 * step)
            logits = lax.dot_general(
                full[Q_, rows, :], full[K_], (((1,), (1,)), ((), ())), preferred_element_type=F32
            ) * scale
            weights = jnp.exp(logits - jnp.max(logits, axis=-1, keepdims=True))
            result = weights / jnp.sum(weights, axis=-1, keepdims=True)
            probs[rows, :] = result
            probs_b[rows, :] = result.astype(BF16)
            return carry

        lax.fori_loop(0, L // (2 * step), body, 0)

    def score_grads():
        def body(i, carry):
            rows = rows_at(i, 2 * step)
            grads = lax.dot_general(
                full[A_, rows, :], full[V_], (((1,), (1,)), ((), ())), preferred_element_type=F32
            )
            prob = probs[rows, :]
            centre = jnp.sum(prob * grads, axis=-1, keepdims=True)
            scores[rows, :] = (scale * prob * (grads - centre)).astype(BF16)
            return carry

        lax.fori_loop(0, L // (2 * step), body, 0)

    def product(t, first, last):
        left = probs_b if t in (AT_, VG_) else scores
        right = full.at[{AT_: V_, VG_: A_, QG_: K_, KG_: Q_}[t]]

        def body(i, carry):
            rows = rows_at(i)
            if t in (AT_, QG_):
                result = jnp.dot(left[rows, :], right[...], preferred_element_type=F32)
            else:
                result = lax.dot_general(
                    left[:, rows], right[...], (((0,), (0,)), ((), ())), preferred_element_type=F32
                )
            outs[t, rows, :] = result.astype(BF16)
            send_back(t, i)
            return carry

        lax.fori_loop(first, last, body, 0)

    def part_of_tokens():
        back_here(AT_)
        for c in tiles:
            for half in range(2):
                lanes = slice(half * 128, half * 128 + 128)
                columns = slice(c * 128, c * 128 + 128)
                one, two = swap_pair(back_att[2 * c, :, lanes], back_att[2 * c + 1, :, lanes], low)
                att[2 * half, :, columns] = one
                att[2 * half + 1, :, columns] = two
        for block in range(3):
            piece = lax.dot_general(
                att[...].reshape(ROWS * POS, D),
                c_in[:, :, block * 256 : block * 256 + 256].reshape(ROWS * POS, 256),
                (((0,), (0,)), ((), ())), preferred_element_type=F32,
            ).astype(BF16)
            w_send[2 * block * D : 2 * block * D + D, :] = piece[:, :128]
            w_send[2 * block * D + D : 2 * block * D + 2 * D, :] = piece[:, 128:]

    counts = ((4, 8), (4, 8))
    firsts, seconds = (z, x), (x * 2 + y, z * 2 + y)

    def in_first(part, other):
        return device(x, y * 4 + other) if part == 0 else device(other, p)

    def in_second(part, other):
        if part == 0:
            return device(other // 2, lax.rem(other, 2) * 4 + z)
        return device(x, lax.rem(other, 2) * 4 + other // 2)

    def block_rows(part):
        return counts[part][1] * SHARES[part]

    def rows_of(part, index):
        return pl.ds(pl.multiple_of(BASES[part] + index * block_rows(part), 16), block_rows(part))

    def share_rows(part, index):
        return pl.ds(pl.multiple_of(index * SHARES[part], 16), SHARES[part])

    def send(src, dst, sems, part, to):
        pltpu.make_async_remote_copy(
            src, dst, w_send_sem.at[sems, part], w_recv_sem.at[sems, part],
            device_id=to, device_id_type=MESH,
        ).start()

    def took(ref, sems, part):
        pltpu.make_async_copy(ref, ref, w_recv_sem.at[sems, part]).wait()

    def others(part, level):
        count = counts[part][level]
        here = (firsts, seconds)[level][part]
        return [(i - 1, lax.rem(here + i, count)) for i in range(1, count)]

    def sum_first_send():
        for part in (1, 0):
            for slot, other in others(part, 0):
                send(
                    w_send.at[rows_of(part, other)], w_first[part].at[slot],
                    0, part, in_first(part, other),
                )

    def sum_second_send():
        for part in (1, 0):
            took(w_first[part], 0, part)
            total = w_send[rows_of(part, firsts[part]), :].astype(F32)
            for slot in range(counts[part][0] - 1):
                total = total + w_first[part][slot].astype(F32)
            w_mid[part][...] = total.astype(BF16)
            for slot, other in others(part, 1):
                send(
                    w_mid[part].at[share_rows(part, other)], w_second[part].at[slot],
                    1, part, in_second(part, other),
                )

    def spread_first_send():
        for part in (1, 0):
            took(w_second[part], 1, part)
            here = share_rows(part, seconds[part])
            total = w_mid[part][here, :].astype(F32)
            for slot in range(counts[part][1] - 1):
                total = total + w_second[part][slot].astype(F32)
            w_block[part][here, :] = total.astype(BF16)
            for slot, other in others(part, 1):
                send(w_block[part].at[here], w_block[part].at[here], 2, part, in_second(part, other))

    own_copies = []

    def spread_second_send():
        for part in (1, 0):
            got = w_block[part].at[pl.ds(0, (counts[part][1] - 1) * SHARES[part])]
            took(got, 2, part)
            there = w_all.at[rows_of(part, firsts[part])]
            for slot, other in others(part, 0):
                send(w_block[part], there, 3, part, in_first(part, other))
            own_copies.append(pltpu.make_async_copy(w_block[part], there, own_sem.at[part]))
            own_copies[-1].start()

    @as_owner
    def _():
        softmax()
        arrived(V_)
        product(AT_, 0, 4)
        arrived(A_)
        product(VG_, 0, 4)
        score_grads()

    part_of_tokens()
    sum_first_send()

    @as_owner
    def _():
        product(QG_, 0, 2)

    sum_second_send()

    @as_owner
    def _():
        product(QG_, 2, 4)
        product(KG_, 0, 2)

    spread_first_send()

    @as_owner
    def _():
        product(KG_, 2, 4)

    spread_second_send()

    for t in (VG_, QG_, KG_):
        back_here(t)
    for part in range(2):
        took(w_all.at[pl.ds(0, (counts[part][0] - 1) * block_rows(part))], 3, part)
    for copy in own_copies:
        copy.wait()

    for t in range(4):
        @pl.when(owner)
        def _():
            sent = stage.at[t, pl.ds(0, H - 1)]
            pltpu.make_async_copy(sent, sent, in_send.at[t]).wait()
            given = outs.at[t, pl.ds(0, L - L // ND)]
            pltpu.make_async_copy(given, given, out_send.at[t]).wait()

        @pl.when(jnp.logical_not(owner))
        def _():
            pltpu.make_async_copy(stage.at[t], stage.at[t], in_send.at[t]).wait()

    for part in range(2):
        first, second = counts[part]
        for sems, rows in enumerate(
            ((first - 1) * second, second - 1, second - 1, (first - 1) * second)
        ):
            sent = w_send.at[pl.ds(0, rows * SHARES[part])]
            pltpu.make_async_copy(sent, sent, w_send_sem.at[sems, part]).wait()


def finish(lengths, back, w_all, q_grads, k_grads, v_grads, w_grad):
    p = lax.axis_index("pos")
    low = lax.broadcasted_iota(jnp.int32, (POS, 2 * HD), 1) < HD
    spots = p * POS + lax.broadcasted_iota(jnp.int32, (POS, 2 * HD), 0)
    for t, result in ((VG_, v_grads), (QG_, q_grads), (KG_, k_grads)):
        for c in range(3):
            columns = slice(c * 128, c * 128 + 128)
            for half in range(2):
                lanes = slice(half * 128, half * 128 + 128)
                pair = swap_pair(
                    back[t - 1, 2 * c, :, lanes], back[t - 1, 2 * c + 1, :, lanes], low
                )
                for i in range(2):
                    row, tile = 2 * half + i, pair[i]
                    if t == QG_:
                        tile = jnp.where(spots < lengths[row], tile, jnp.zeros((), BF16))
                    result[row, :, columns] = tile
    for c in range(3):
        w_grad[:, c * 128 : c * 128 + 128] = w_all[c * D : c * D + D, :].astype(F32)


def per_device(queries, keys, values, out_weight, cotangent, lengths):
    any_space = pl.BlockSpec(memory_space=pl.ANY)
    smem = pl.BlockSpec(memory_space=pltpu.SMEM)
    vmem = pltpu.VMEM
    dma = pltpu.SemaphoreType.DMA
    back, w_all = pl.pallas_call(
        kernel,
        out_shape=(
            jax.ShapeDtypeStruct((3, H, POS, TILE), BF16),
            jax.ShapeDtypeStruct((ND * SLICE, 128), BF16),
        ),
        in_specs=[smem] + [any_space] * 5,
        out_specs=(any_space,) * 2,
        scratch_shapes=[
            vmem((ROWS, POS, D), BF16),
            vmem((ROWS, POS, D), BF16),
            vmem((ROWS, POS, D), BF16),
            vmem((ROWS, POS, D), BF16),
            vmem((D, D), BF16),
            vmem((4, H, POS, TILE), BF16),
            vmem((4, L, WIDE), BF16),
            vmem((L, L), F32),
            vmem((L, L), BF16),
            vmem((L, L), BF16),
            vmem((4, L, WIDE), BF16),
            vmem((H, POS, TILE), BF16),
            vmem((ROWS, POS, D), BF16),
            vmem((ND * SLICE, 128), BF16),
            vmem((3, 8 * SHARES[0], 128), BF16),
            vmem((3, 8 * SHARES[1], 128), BF16),
            vmem((8 * SHARES[0], 128), BF16),
            vmem((8 * SHARES[1], 128), BF16),
            vmem((7, SHARES[0], 128), BF16),
            vmem((7, SHARES[1], 128), BF16),
            vmem((8 * SHARES[0], 128), BF16),
            vmem((8 * SHARES[1], 128), BF16),
            dma((5,)), dma((4,)), dma((4,)), dma((4,)), dma((4,)), dma((4, 2)), dma((4, 2)), dma((2,)),
        ],
        compiler_params=pltpu.CompilerParams(
            collective_id=0, has_side_effects=True, vmem_limit_bytes=58 * 2**20
        ),
        cost_estimate=pl.CostEstimate(
            flops=14 * L**3, bytes_accessed=12 * 2**20, transcendentals=L * L
        ),
    )(lengths, queries, keys, values, cotangent, out_weight)
    local = jax.ShapeDtypeStruct((ROWS, POS, D), BF16)
    grads = pl.BlockSpec((ROWS, POS, 384), lambda i: (0, 0, i))
    return pl.pallas_call(
        finish,
        out_shape=(local, local, local, jax.ShapeDtypeStruct((D, D), F32)),
        grid=(2,),
        in_specs=[
            smem,
            pl.BlockSpec((3, 6, POS, TILE), lambda i: (0, i, 0, 0)),
            pl.BlockSpec((2304, 128), lambda i: (i, 0)),
        ],
        out_specs=(grads, grads, grads, pl.BlockSpec((D, 384), lambda i: (0, i))),
        compiler_params=pltpu.CompilerParams(vmem_limit_bytes=60 * 2**20),
    )(lengths, back, w_all)


def solution(mesh):
    tokens = P(("batch", "row"), "pos", None)
    return jax.shard_map(
        per_device,
        mesh=mesh,
        in_specs=(tokens, tokens, tokens, P(), tokens, P(("batch", "row"))),
        out_specs=(tokens, tokens, tokens, P("batch", None)),
        check_vma=False,
    )
```

time: 154 us -> 133 us (0.86)
  Pallas kernels: 145 us -> 130 us
  local copies, waits for them, and re-layouts: 6.57 us -> 0 us
    pallas_call x1 -> x2, Pallas kernels: 145 us -> 130 us  [the longest x1 126 us: per_device(): pl.pallas_call(kernel, out_shape=(jax.ShapeDtypeStruct((3, H, POS, TILE),...]
    unnamed x8 -> x0, local copies, waits for them, and re-layouts: 6.57 us -> none
where the time goes in v5:
time: 133 us; the launch traced here: 131 us
  Pallas kernels  130 us (98%)
    pallas_call x1, Pallas kernels, per_device(): pl.pallas_call(kernel, out_shape=(jax.ShapeDtypeStruct((3, H, POS, TILE),...  126 us
    pallas_call x1, Pallas kernels, per_device(): pl.pallas_call(finish, out_shape=(local, local, local, jax.ShapeDtypeStru...  3.96 us

profile of v5, /device:TPU:16, one launch (start us, length us, event | category | flops | bytes accessed | tf_op | source)
XLA Modules:
  0.0 131.0 jit_solution(8075779849223760865)
XLA Ops:
  0.6 126.4 %shard_map.93 = (bf16[3,12,128,256]{3,2,1,0:T(8,128)(2,1)}, bf16[4608,128]{1,0:T(8,128)(2,1)}) custom-call(s32[4]{0:T(128)} %lengths.3, bf16[4,128,768]{2,1,0:T(8,128)(2,1)} %q_hbm.1, bf16[4,128,768]{2,1,0:T(8,128)(2,1)} %k_hbm.1, bf16[4,128,768]{2,1,0:T(8,128)(2,1)} %v_hbm.1, bf16[4,128,768]{2,1,0:T(8,128)(2,1)} %c_hbm.1, bf16[768,768]{1,0:T(8,128)(2,1)} %w_hbm.1), custom_call_target="tpu_custom_call" | custom-call | flops 15032385536 | bytes 12582912 | tf_op jit(solution)/shard_map/pallas_call | solution.py:428
  127.1 4.0 %shard_map.94 = (bf16[4,128,768]{2,1,0:T(8,128)(2,1)}, bf16[4,128,768]{2,1,0:T(8,128)(2,1)}, bf16[4,128,768]{2,1,0:T(8,128)(2,1)}, f32[768,768]{1,0:T(8,128)}) custom-call(s32[4]{0:T(128)} %lengths.3, bf16[3,12,128,256]{3,2,1,0:T(8,128)(2,1)} %get-tuple-element.6.back, bf16[4608,128]{1,0:T(8,128)(2,1)} %get-tuple-element.7.w_all), custom_call_target="tpu_custom_call" | custom-call | tf_op jit(solution)/shard_map/pallas_call | solution.py:470

commit v6 on v5

--- a/solution.py
+++ b/solution.py
@@ -19,8 +19,9 @@
 TILE = ROWS * HD
 WIDE = TILE * NX
 SLICE = D * D // 128 // ND
-SHARES = (80, 64)
-BASES = (0, ND * SHARES[0])
+SHARES = (48, 48, 48)
+PARTS = (0, 1, 2)
+BASES = (0, ND * SHARES[0], ND * (SHARES[0] + SHARES[1]))
 HEADS_X = H // NX
 MESH = pl.DeviceIdType.MESH
 F32 = jnp.float32
@@ -40,12 +41,12 @@
     lengths, q_hbm, k_hbm, v_hbm, c_hbm, w_hbm,
     back, w_all,
     q_in, k_in, v_in, c_in, w_in, stage, full, probs, probs_b, scores, outs, back_att,
-    att, w_send, w_first_a, w_first_b, w_mid_a, w_mid_b, w_second_a, w_second_b,
-    w_block_a, w_block_b,
+    att, w_send, w_first_a, w_first_b, w_first_c, w_mid_a, w_mid_b, w_mid_c,
+    w_second_a, w_second_b, w_second_c, w_block_a, w_block_b, w_block_c,
     load_sem, in_send, in_recv, out_send, out_recv, w_send_sem, w_recv_sem, own_sem,
 ):
-    w_first, w_mid = (w_first_a, w_first_b), (w_mid_a, w_mid_b)
-    w_second, w_block = (w_second_a, w_second_b), (w_block_a, w_block_b)
+    w_first, w_mid = (w_first_a, w_first_b, w_first_c), (w_mid_a, w_mid_b, w_mid_c)
+    w_second, w_block = (w_second_a, w_second_b, w_second_c), (w_block_a, w_block_b, w_block_c)
     x = lax.axis_index("row")
     p = lax.axis_index("pos")
     core = lax.rem(lax.axis_index("batch"), 2)
@@ -262,16 +263,20 @@
             w_send[2 * block * D : 2 * block * D + D, :] = piece[:, :128]
             w_send[2 * block * D + D : 2 * block * D + 2 * D, :] = piece[:, 128:]
 
-    counts = ((4, 8), (4, 8))
-    firsts, seconds = (z, x), (x * 2 + y, z * 2 + y)
+    counts = ((4, 8), (4, 8), (2, 16))
+    firsts, seconds = (z, x, y), (x * 2 + y, z * 2 + y, x * 4 + z)
 
     def in_first(part, other):
-        return device(x, y * 4 + other) if part == 0 else device(other, p)
+        if part == 0:
+            return device(x, y * 4 + other)
+        return device(other, p) if part == 1 else device(x, other * 4 + z)
 
     def in_second(part, other):
         if part == 0:
             return device(other // 2, lax.rem(other, 2) * 4 + z)
-        return device(x, lax.rem(other, 2) * 4 + other // 2)
+        if part == 1:
+            return device(x, lax.rem(other, 2) * 4 + other // 2)
+        return device(other // 4, y * 4 + lax.rem(other, 4))
 
     def block_rows(part):
         return counts[part][1] * SHARES[part]
@@ -297,7 +302,7 @@
         return [(i - 1, lax.rem(here + i, count)) for i in range(1, count)]
 
     def sum_first_send():
-        for part in (1, 0):
+        for part in PARTS:
             for slot, other in others(part, 0):
                 send(
                     w_send.at[rows_of(part, other)], w_first[part].at[slot],
@@ -305,7 +310,7 @@
                 )
 
     def sum_second_send():
-        for part in (1, 0):
+        for part in PARTS:
             took(w_first[part], 0, part)
             total = w_send[rows_of(part, firsts[part]), :].astype(F32)
             for slot in range(counts[part][0] - 1):
@@ -318,7 +323,7 @@
                 )
 
     def spread_first_send():
-        for part in (1, 0):
+        for part in PARTS:
             took(w_second[part], 1, part)
             here = share_rows(part, seconds[part])
             total = w_mid[part][here, :].astype(F32)
@@ -331,7 +336,7 @@
     own_copies = []
 
     def spread_second_send():
-        for part in (1, 0):
+        for part in PARTS:
             got = w_block[part].at[pl.ds(0, (counts[part][1] - 1) * SHARES[part])]
             took(got, 2, part)
             there = w_all.at[rows_of(part, firsts[part])]
@@ -346,34 +351,33 @@
         arrived(V_)
         product(AT_, 0, 4)
         arrived(A_)
-        product(VG_, 0, 4)
         score_grads()
+        product(QG_, 0, 4)
 
     part_of_tokens()
     sum_first_send()
 
     @as_owner
     def _():
-        product(QG_, 0, 2)
+        product(KG_, 0, 2)
 
     sum_second_send()
-
-    @as_owner
-    def _():
-        product(QG_, 2, 4)
-        product(KG_, 0, 2)
-
-    spread_first_send()
 
     @as_owner
     def _():
         product(KG_, 2, 4)
 
+    spread_first_send()
+
+    @as_owner
+    def _():
+        product(VG_, 0, 4)
+
     spread_second_send()
 
     for t in (VG_, QG_, KG_):
         back_here(t)
-    for part in range(2):
+    for part in PARTS:
         took(w_all.at[pl.ds(0, (counts[part][0] - 1) * block_rows(part))], 3, part)
     for copy in own_copies:
         copy.wait()
@@ -390,7 +394,7 @@
         def _():
             pltpu.make_async_copy(stage.at[t], stage.at[t], in_send.at[t]).wait()
 
-    for part in range(2):
+    for part in PARTS:
         first, second = counts[part]
         for sems, rows in enumerate(
             ((first - 1) * second, second - 1, second - 1, (first - 1) * second)
@@ -450,13 +454,17 @@
             vmem((ND * SLICE, 128), BF16),
             vmem((3, 8 * SHARES[0], 128), BF16),
             vmem((3, 8 * SHARES[1], 128), BF16),
+            vmem((1, 16 * SHARES[2], 128), BF16),
             vmem((8 * SHARES[0], 128), BF16),
             vmem((8 * SHARES[1], 128), BF16),
+            vmem((16 * SHARES[2], 128), BF16),
             vmem((7, SHARES[0], 128), BF16),
             vmem((7, SHARES[1], 128), BF16),
+            vmem((15, SHARES[2], 128), BF16),
             vmem((8 * SHARES[0], 128), BF16),
             vmem((8 * SHARES[1], 128), BF16),
-            dma((5,)), dma((4,)), dma((4,)), dma((4,)), dma((4,)), dma((4, 2)), dma((4, 2)), dma((2,)),
+            vmem((16 * SHARES[2], 128), BF16),
+            dma((5,)), dma((4,)), dma((4,)), dma((4,)), dma((4,)), dma((4, 3)), dma((4, 3)), dma((3,)),
         ],
         compiler_params=pltpu.CompilerParams(
             collective_id=0, has_side_effects=True, vmem_limit_bytes=58 * 2**20

time: 133 us -> 130 us (0.977)
  Pallas kernels: 130 us -> 127 us
    pallas_call x1, Pallas kernels: 126 us -> 123 us  [per_device(): pl.pallas_call(kernel, out_shape=(jax.ShapeDtypeStruct((3, H, POS, TILE),...]
where the time goes in v6:
time: 130 us; the launch traced here: 128 us
  Pallas kernels  127 us (98%)
    pallas_call x1, Pallas kernels, per_device(): pl.pallas_call(kernel, out_shape=(jax.ShapeDtypeStruct((3, H, POS, TILE),...  123 us
    pallas_call x1, Pallas kernels, per_device(): pl.pallas_call(finish, out_shape=(local, local, local, jax.ShapeDtypeStru...  3.96 us

profile of v6, /device:TPU:16, one launch (start us, length us, event | category | flops | bytes accessed | tf_op | source)
XLA Modules:
  0.0 127.8 jit_solution(17945011126978432032)
XLA Ops:
  0.6 123.2 %shard_map.93 = (bf16[3,12,128,256]{3,2,1,0:T(8,128)(2,1)}, bf16[4608,128]{1,0:T(8,128)(2,1)}) custom-call(s32[4]{0:T(128)} %lengths.3, bf16[4,128,768]{2,1,0:T(8,128)(2,1)} %q_hbm.1, bf16[4,128,768]{2,1,0:T(8,128)(2,1)} %k_hbm.1, bf16[4,128,768]{2,1,0:T(8,128)(2,1)} %v_hbm.1, bf16[4,128,768]{2,1,0:T(8,128)(2,1)} %c_hbm.1, bf16[768,768]{1,0:T(8,128)(2,1)} %w_hbm.1), custom_call_target="tpu_custom_call" | custom-call | flops 15032385536 | bytes 12582912 | tf_op jit(solution)/shard_map/pallas_call | solution.py:432
  123.9 4.0 %shard_map.94 = (bf16[4,128,768]{2,1,0:T(8,128)(2,1)}, bf16[4,128,768]{2,1,0:T(8,128)(2,1)}, bf16[4,128,768]{2,1,0:T(8,128)(2,1)}, f32[768,768]{1,0:T(8,128)}) custom-call(s32[4]{0:T(128)} %lengths.3, bf16[3,12,128,256]{3,2,1,0:T(8,128)(2,1)} %get-tuple-element.6.back, bf16[4608,128]{1,0:T(8,128)(2,1)} %get-tuple-element.7.w_all), custom_call_target="tpu_custom_call" | custom-call | tf_op jit(solution)/shard_map/pallas_call | solution.py:478

commit v7 on v6

--- a/solution.py
+++ b/solution.py
@@ -101,7 +101,7 @@
 
     def send_heads(t):
         def body(i, carry):
-            h = lax.rem(i + HEADS_X * x, H)
+            h = lax.rem(i + HEADS_X * (x + 2), H)
             hx, hp = owner_of(h)
             place = full.at[
                 t, pl.ds(pl.multiple_of(p * POS, POS), POS), pl.ds(pl.multiple_of(x * TILE, TILE), TILE)

time: 130 us -> 128 us (0.985); the launches traced: 128 us -> 128 us
  no operation moved by 1% of the time
where the time goes in v7:
time: 128 us
  Pallas kernels  127 us (99%)
    pallas_call x1, Pallas kernels, per_device(): pl.pallas_call(kernel, out_shape=(jax.ShapeDtypeStruct((3, H, POS, TILE),...  123 us
    pallas_call x1, Pallas kernels, per_device(): pl.pallas_call(finish, out_shape=(local, local, local, jax.ShapeDtypeStru...  3.96 us

profile of v7, /device:TPU:16, one launch (start us, length us, event | category | flops | bytes accessed | tf_op | source)
XLA Modules:
  0.0 127.6 jit_solution(7931303121981380015)
XLA Ops:
  0.6 123.0 %shard_map.93 = (bf16[3,12,128,256]{3,2,1,0:T(8,128)(2,1)}, bf16[4608,128]{1,0:T(8,128)(2,1)}) custom-call(s32[4]{0:T(128)} %lengths.3, bf16[4,128,768]{2,1,0:T(8,128)(2,1)} %q_hbm.1, bf16[4,128,768]{2,1,0:T(8,128)(2,1)} %k_hbm.1, bf16[4,128,768]{2,1,0:T(8,128)(2,1)} %v_hbm.1, bf16[4,128,768]{2,1,0:T(8,128)(2,1)} %c_hbm.1, bf16[768,768]{1,0:T(8,128)(2,1)} %w_hbm.1), custom_call_target="tpu_custom_call" | custom-call | flops 15032385536 | bytes 12582912 | tf_op jit(solution)/shard_map/pallas_call | solution.py:432
  123.7 4.0 %shard_map.94 = (bf16[4,128,768]{2,1,0:T(8,128)(2,1)}, bf16[4,128,768]{2,1,0:T(8,128)(2,1)}, bf16[4,128,768]{2,1,0:T(8,128)(2,1)}, f32[768,768]{1,0:T(8,128)}) custom-call(s32[4]{0:T(128)} %lengths.3, bf16[3,12,128,256]{3,2,1,0:T(8,128)(2,1)} %get-tuple-element.6.back, bf16[4608,128]{1,0:T(8,128)(2,1)} %get-tuple-element.7.w_all), custom_call_target="tpu_custom_call" | custom-call | tf_op jit(solution)/shard_map/pallas_call | solution.py:478

commit v8 on v7

--- a/solution.py
+++ b/solution.py
@@ -408,7 +408,7 @@
     low = lax.broadcasted_iota(jnp.int32, (POS, 2 * HD), 1) < HD
     spots = p * POS + lax.broadcasted_iota(jnp.int32, (POS, 2 * HD), 0)
     for t, result in ((VG_, v_grads), (QG_, q_grads), (KG_, k_grads)):
-        for c in range(3):
+        for c in range(6):
             columns = slice(c * 128, c * 128 + 128)
             for half in range(2):
                 lanes = slice(half * 128, half * 128 + 128)
@@ -420,7 +420,7 @@
                     if t == QG_:
                         tile = jnp.where(spots < lengths[row], tile, jnp.zeros((), BF16))
                     result[row, :, columns] = tile
-    for c in range(3):
+    for c in range(6):
         w_grad[:, c * 128 : c * 128 + 128] = w_all[c * D : c * D + D, :].astype(F32)
 
 
@@ -474,17 +474,17 @@
         ),
     )(lengths, queries, keys, values, cotangent, out_weight)
     local = jax.ShapeDtypeStruct((ROWS, POS, D), BF16)
-    grads = pl.BlockSpec((ROWS, POS, 384), lambda i: (0, 0, i))
+    grads = pl.BlockSpec((ROWS, POS, D), lambda i: (0, 0, i))
     return pl.pallas_call(
         finish,
         out_shape=(local, local, local, jax.ShapeDtypeStruct((D, D), F32)),
-        grid=(2,),
+        grid=(1,),
         in_specs=[
             smem,
-            pl.BlockSpec((3, 6, POS, TILE), lambda i: (0, i, 0, 0)),
-            pl.BlockSpec((2304, 128), lambda i: (i, 0)),
+            pl.BlockSpec((3, H, POS, TILE), lambda i: (0, i, 0, 0)),
+            pl.BlockSpec((6 * D, 128), lambda i: (i, 0)),
         ],
-        out_specs=(grads, grads, grads, pl.BlockSpec((D, 384), lambda i: (0, i))),
+        out_specs=(grads, grads, grads, pl.BlockSpec((D, D), lambda i: (0, i))),
         compiler_params=pltpu.CompilerParams(vmem_limit_bytes=60 * 2**20),
     )(lengths, back, w_all)
 

time: 128 us -> 129 us (level)
  no operation moved by 1% of the time
where the time goes in v8:
time: 129 us
  Pallas kernels  128 us (99%)
    pallas_call x1, Pallas kernels, per_device(): pl.pallas_call(kernel, out_shape=(jax.ShapeDtypeStruct((3, H, POS, TILE),...  123 us
    pallas_call x1, Pallas kernels, per_device(): pl.pallas_call(finish, out_shape=(local, local, local, jax.ShapeDtypeStru...  4.84 us

profile of v8, /device:TPU:16, one launch (start us, length us, event | category | flops | bytes accessed | tf_op | source)
XLA Modules:
  0.0 128.5 jit_solution(11779193940654618687)
XLA Ops:
  0.6 123.0 %shard_map.93 = (bf16[3,12,128,256]{3,2,1,0:T(8,128)(2,1)}, bf16[4608,128]{1,0:T(8,128)(2,1)}) custom-call(s32[4]{0:T(128)} %lengths.3, bf16[4,128,768]{2,1,0:T(8,128)(2,1)} %q_hbm.1, bf16[4,128,768]{2,1,0:T(8,128)(2,1)} %k_hbm.1, bf16[4,128,768]{2,1,0:T(8,128)(2,1)} %v_hbm.1, bf16[4,128,768]{2,1,0:T(8,128)(2,1)} %c_hbm.1, bf16[768,768]{1,0:T(8,128)(2,1)} %w_hbm.1), custom_call_target="tpu_custom_call" | custom-call | flops 15032385536 | bytes 12582912 | tf_op jit(solution)/shard_map/pallas_call | solution.py:432
  123.7 4.8 %shard_map.94 = (bf16[4,128,768]{2,1,0:T(8,128)(2,1)}, bf16[4,128,768]{2,1,0:T(8,128)(2,1)}, bf16[4,128,768]{2,1,0:T(8,128)(2,1)}, f32[768,768]{1,0:T(8,128)}) custom-call(s32[4]{0:T(128)} %lengths.3, bf16[3,12,128,256]{3,2,1,0:T(8,128)(2,1)} %get-tuple-element.6.back, bf16[4608,128]{1,0:T(8,128)(2,1)} %get-tuple-element.7.w_all), custom_call_target="tpu_custom_call" | custom-call | tf_op jit(solution)/shard_map/pallas_call | solution.py:478
